TPU v7x, 256 devices: a whole 4x4x8 slice. The times are simulated.
256 devices in a mesh: dom: 64 (over y, x_hi, z), rep: 4 (over x_lo, core).
Axes of the slice: x: 4 (x_hi: 2, x_lo: 2; x = x_hi * 2 + x_lo), y: 4, z: 8, core: 2. Of those that a mesh axis runs over, the one named last changes fastest.
Arguments:
- entities: float32 [32768, 384], P('dom'), may hold values from -1.8 to 1.8
- entity_state: float32 [32768], P('dom'), may hold values from 0.01 to 1
- relations: float32 [7424, 384], P(('dom', 'rep')), may hold values from -1.8 to 1.8
- relation_state: float32 [7424], P(('dom', 'rep')), may hold values from 0.01 to 1
- head_ids: int32 [512000], P(('dom', 'rep')), may hold values from 0 to 511
- relation_ids: int32 [512000], P(('dom', 'rep')), may hold values from 0 to 7423
- tail_ids: int32 [512000], P(('dom', 'rep')), may hold values from 0 to 511
- head_negatives: int32 [512, 1000], P(('dom', 'rep')), may hold values from 0 to 511
- tail_negatives: int32 [512, 1000], P(('dom', 'rep')), may hold values from 0 to 511
- bucket_sizes: int32 [64], P('dom'), may hold values from 1000 to 8000, as said below
- plan: int32 [64], replicated, may hold values from 0 to 63, as said below
Outputs:
- new_entities: float32 [32768, 384], P('dom')
- new_entity_state: float32 [32768], P('dom')
- new_relations: float32 [7424, 384], P(('dom', 'rep'))
- new_relation_state: float32 [7424], P(('dom', 'rep'))
Inputs may be any that keep to these rules, and one draw needn't show every extreme that they name: `bucket_sizes`: the largest bucket is full: some bucket has 8000 live slots in every draw; each has at least an eighth of that. plan[p] = p XOR m for one m, the same for all p, with 1 <= m < 64; so plan is its own inverse and has no fixed point.
All inputs are finite; a program needn't handle non-finite values.
Results may differ from a plain program's by a relative error of at most 0.0034.
Values may be sent and summed in bfloat16 or wider, within the bound.
A program may use at most 128 MiB of HBM per device.

v0:
```python
import jax
import jax.numpy as jnp
from jax import lax
from jax.sharding import PartitionSpec as P

LEARN = 0.1


def swapped(block, axis, distance):
    count = lax.axis_size(axis)
    route = []
    for low in range(count):
        high = low | 1 << distance
        if high != low and high < count:
            route += [(low, high), (high, low)]
    return lax.ppermute(block, axis, route)


def split_halves(rows):
    half = rows.shape[1] // 2
    return (rows[:, :half], rows[:, half:])


def edge_gradients(head_rows, relation_rows, tail_rows, head_negs, tail_negs, active):
    head_full = head_rows.astype(jnp.float32)
    tail_full = tail_rows.astype(jnp.float32)
    head_real, head_imag = split_halves(head_full)
    rel_real, rel_imag = split_halves(relation_rows.astype(jnp.float32))
    tail_real, tail_imag = split_halves(tail_full)
    query = jnp.concatenate(
        [head_real * rel_real - head_imag * rel_imag, head_real * rel_imag + head_imag * rel_real],
        axis=1,
    )
    probe = jnp.concatenate(
        [rel_real * tail_real + rel_imag * tail_imag, rel_real * tail_imag - rel_imag * tail_real],
        axis=1,
    )
    positive = jnp.sum(query * tail_full, axis=1)
    query_low = query.astype(jnp.bfloat16)
    probe_low = probe.astype(jnp.bfloat16)
    inner = (((1,), (1,)), ((), ()))
    outer = (((0,), (0,)), ((), ()))
    tail_scores = lax.dot_general(query_low, tail_negs, inner, preferred_element_type=jnp.float32)
    head_scores = lax.dot_general(probe_low, head_negs, inner, preferred_element_type=jnp.float32)
    samples = tail_negs.shape[0]
    pos_weight = -active * jax.nn.sigmoid(-positive)
    scaling = (active / samples)[:, None]
    tail_weight = (jax.nn.sigmoid(tail_scores) * scaling).astype(jnp.bfloat16)
    head_weight = (jax.nn.sigmoid(head_scores) * scaling).astype(jnp.bfloat16)
    query_grad = pos_weight[:, None] * tail_full + jnp.dot(
        tail_weight, tail_negs, preferred_element_type=jnp.float32
    )
    probe_grad = jnp.dot(head_weight, head_negs, preferred_element_type=jnp.float32)
    tail_neg_grad = lax.dot_general(
        tail_weight, query_low, outer, preferred_element_type=jnp.float32
    )
    head_neg_grad = lax.dot_general(
        head_weight, probe_low, outer, preferred_element_type=jnp.float32
    )
    qg_real, qg_imag = split_halves(query_grad)
    pg_real, pg_imag = split_halves(probe_grad)
    head_grad = jnp.concatenate(
        [qg_real * rel_real + qg_imag * rel_imag, qg_imag * rel_real - qg_real * rel_imag], axis=1
    )
    tail_grad = (
        jnp.concatenate(
            [pg_real * rel_real - pg_imag * rel_imag, pg_real * rel_imag + pg_imag * rel_real],
            axis=1,
        )
        + pos_weight[:, None] * query
    )
    relation_grad = jnp.concatenate(
        [
            qg_real * head_real + qg_imag * head_imag + pg_real * tail_real + pg_imag * tail_imag,
            qg_imag * head_real - qg_real * head_imag + pg_real * tail_imag - pg_imag * tail_real,
        ],
        axis=1,
    )
    return (head_grad, tail_grad, relation_grad, head_neg_grad, tail_neg_grad)


def adagrad(param, state, grad):
    new_state = state + jnp.mean(grad * grad, axis=1)
    return (param - LEARN * grad / jnp.sqrt(new_state)[:, None], new_state)


def flag_bit(partner_mask, which):
    return jnp.bitwise_and(jnp.right_shift(partner_mask, which), 1) == 1


def to_partner(values, partner_mask, bit_order):
    for which in bit_order:
        moved = swapped(values, "dom", which)
        values = jnp.where(flag_bit(partner_mask, which), moved, values)
    return values


def back_whole(values, partner_mask, bit_order):
    for which in bit_order:
        moved = swapped(values.astype(jnp.bfloat16), "dom", which).astype(values.dtype)
        values = jnp.where(flag_bit(partner_mask, which), moved, values)
    return values


def fetch_relations(table_low, relation_ids):
    whole_table = lax.all_gather(table_low, ("dom", "rep"), axis=0, tiled=True)
    return jnp.take(whole_table, relation_ids, axis=0)


def ranged_sum(values, row_ids, row_count):
    local_ids = row_ids
    inside = (local_ids >= 0) & (local_ids < row_count)
    local_ids = jnp.where(inside, local_ids, row_count)
    summed = jax.ops.segment_sum(values, local_ids, num_segments=row_count + 1)
    return summed[:row_count]


def local(
    entities,
    entity_state,
    relations,
    relation_state,
    head_ids,
    relation_ids,
    tail_ids,
    head_negatives,
    tail_negatives,
    bucket_sizes,
    plan,
):
    ent_rows = entities.shape[0]
    width = entities.shape[1]
    edge_slots = head_ids.shape[0]
    block_rows = edge_slots // head_negatives.shape[0]
    bit_count = lax.axis_size("dom").bit_length() - 1
    bit_order = list(range(bit_count))
    partner_mask = plan[0]
    own_low = entities.astype(jnp.bfloat16)
    partner_low = to_partner(own_low, partner_mask, bit_order)
    relation_rows = fetch_relations(relations.astype(jnp.bfloat16), relation_ids)
    rep_index = lax.axis_index("rep")
    slots = rep_index * edge_slots + jnp.arange(edge_slots, dtype=jnp.int32)
    active_all = (slots < bucket_sizes[0]).astype(jnp.float32)
    head_sum = jnp.zeros((ent_rows, width), jnp.float32)
    tail_sum = jnp.zeros((ent_rows, width), jnp.float32)
    relation_parts = []
    for block in range(head_negatives.shape[0]):
        lower = block * block_rows
        upper = lower + block_rows
        heads_here = head_ids[lower:upper]
        tails_here = tail_ids[lower:upper]
        negs_head = head_negatives[block]
        negs_tail = tail_negatives[block]
        grads = edge_gradients(
            jnp.take(own_low, heads_here, axis=0),
            relation_rows[lower:upper],
            jnp.take(partner_low, tails_here, axis=0),
            jnp.take(own_low, negs_head, axis=0),
            jnp.take(partner_low, negs_tail, axis=0),
            active_all[lower:upper],
        )
        head_grad, tail_grad, relation_grad, head_neg_grad, tail_neg_grad = grads
        head_sum = (
            head_sum
            + jax.ops.segment_sum(head_grad, heads_here, num_segments=ent_rows)
            + jax.ops.segment_sum(head_neg_grad, negs_head, num_segments=ent_rows)
        )
        tail_sum = (
            tail_sum
            + jax.ops.segment_sum(tail_grad, tails_here, num_segments=ent_rows)
            + jax.ops.segment_sum(tail_neg_grad, negs_tail, num_segments=ent_rows)
        )
        relation_parts.append(relation_grad)
    relation_delta = jnp.concatenate(relation_parts, axis=0)
    returned = back_whole(tail_sum, partner_mask, bit_order)
    summed = lax.psum((head_sum + returned).astype(jnp.bfloat16), "rep").astype(jnp.float32)
    new_entities, new_entity_state = adagrad(entities, entity_state, summed)
    shard_rows = relations.shape[0]
    relation_sum = lax.psum_scatter(
        ranged_sum(relation_delta, relation_ids, shard_rows * lax.axis_size(("dom", "rep"))),
        ("dom", "rep"),
        scatter_dimension=0,
        tiled=True,
    )
    new_relations, new_relation_state = adagrad(relations, relation_state, relation_sum)
    return (new_entities, new_entity_state, new_relations, new_relation_state)


def solution(mesh):
    placed = (
        P("dom", None),
        P("dom"),
        P(("dom", "rep"), None),
        P(("dom", "rep")),
        P(("dom", "rep")),
        P(("dom", "rep")),
        P(("dom", "rep")),
        P(("dom", "rep"), None),
        P(("dom", "rep"), None),
        P("dom"),
        P(),
    )
    return jax.shard_map(
        local,
        mesh=mesh,
        in_specs=placed,
        out_specs=(P("dom", None), P("dom"), P(("dom", "rep"), None), P(("dom", "rep"))),
        check_vma=False,
    )
```

profile of v0, /device:TPU:1, one launch (start us, length us, event | category | flops | bytes accessed | tf_op | source)
XLA Modules:
  0.0 1569.1 jit_solution(3287765176077819952)
XLA Ops:
  9.9 2.6 collective-permute-start
  17.8 5.0 gather_fusion.4
  22.8 5.0 gather_fusion.8
  27.9 4.2 gather_fusion.5
  32.1 4.2 gather_fusion.1
  36.6 3.1 collective-permute-start.1
  39.7 19.0 %collective-permute-done.1 = bf16[512,384]{1,0:T(8,128)(2,1)S(1)} collective-permute-done((bf16[512,384]{1,0:T(8,128)(2,1)S(1)}, bf16[512,384]{1,0:T(8,128)(2,1)S(1)}, u32[]{:S(2)}, u32[]{:S(2)}) %collective-permute-start.1) | collective-permute-done | bytes 393248 | tf_op jit(solution)/shard_map/ppermute | solution.py:16
  58.7 5.4 collective-permute-start.2
  64.1 18.3 %collective-permute-done.2 = bf16[512,384]{1,0:T(8,128)(2,1)S(1)} collective-permute-done((bf16[512,384]{1,0:T(8,128)(2,1)S(1)}, bf16[512,384]{1,0:T(8,128)(2,1)S(1)}, u32[]{:S(2)}, u32[]{:S(2)}) %collective-permute-start.2) | collective-permute-done | bytes 393248 | tf_op jit(solution)/shard_map/ppermute | solution.py:16
  83.0 10.5 collective-permute-done.3
  96.0 5.8 collective-permute-done.4
  105.1 5.7 collective-permute-done.5
  110.9 4.2 gather_fusion.6
  115.1 4.2 gather_fusion.2
  119.2 5.0 gather_fusion.7
  124.2 5.0 gather_fusion.3
  132.0 317.0 %all-gather.3.cloned.1.call-done = bf16[256,29,384]{2,1,0:T(8,128)(2,1)} async-done(((bf16[1,29,384]{2,1,0:T(8,128)(2,1)}), bf16[256,29,384]{2,1,0:T(8,128)(2,1)}) %all-gather.3.cloned.1.call-update) | async-done | bytes 5701648 | tf_op jit(solution)/shard_map/all_gather | solution.py:106
  449.0 9.5 reshape.223
  458.5 10.8 gather_fusion
  479.2 2.5 fusion.65
  481.7 2.5 multiply_add_fusion.1
  486.0 2.5 fusion.68
  488.5 2.5 multiply_add_fusion
  491.0 8.5 scatter_custom_fusion.5
  499.5 8.0 scatter_custom_fusion.7
  507.5 4.6 multiply_add_fusion.6
  516.4 1.9 multiply_subtract_fusion.2
  518.8 2.2 multiply_add_fusion.8
  524.2 2.0 multiply_subtract_fusion.3
  526.2 9.4 scatter_custom_fusion.4
  535.7 2.4 add.167
  538.1 10.2 scatter_custom_fusion.6
  550.7 6.7 collective-permute-done.6
  559.3 17.4 %collective-permute-done.7 = bf16[512,384]{1,0:T(8,128)(2,1)S(1)} collective-permute-done((bf16[512,384]{1,0:T(8,128)(2,1)S(1)}, bf16[512,384]{1,0:T(8,128)(2,1)S(1)}, u32[]{:S(2)}, u32[]{:S(2)}) %collective-permute-start.7) | collective-permute-done | bytes 393248 | tf_op jit(solution)/shard_map/ppermute | solution.py:16
  576.9 4.7 collective-permute-start.8
  581.6 17.2 %collective-permute-done.8 = bf16[512,384]{1,0:T(8,128)(2,1)S(1)} collective-permute-done((bf16[512,384]{1,0:T(8,128)(2,1)S(1)}, bf16[512,384]{1,0:T(8,128)(2,1)S(1)}, u32[]{:S(2)}, u32[]{:S(2)}) %collective-permute-start.8) | collective-permute-done | bytes 393248 | tf_op jit(solution)/shard_map/ppermute | solution.py:16
  598.9 4.7 collective-permute-start.9
  603.7 2.5 multiply_add_fusion.2
  606.2 2.6 multiply_add_fusion.3
  608.9 20.0 %scatter_custom_fusion.8 = f32[7425,384]{1,0:T(8,128)} fusion(s32[2000]{0:T(1024)S(1)} %get-tuple-element.41, f32[]{:T(128)} %constant.39.clone.1, f32[1000,192]{1,0:T(8,128)} %get-tuple-element.18, f32[]{:T(128)} %constant.95, f32[1000,192]{1,0:T(8,128)} %get-tuple-element.17, f32[1000,192]{1,0:T(8,128)} %get-tuple-element.16, ...), kind=kCustom, calls=%fused_computation.18 | custom fusion | flops 3072000 | bytes 14476808 | tf_op jit(solution)/shard_map/scatter-add | solution.py:114
  628.9 9.1 slice.178
  639.2 694.3 %fusion = f32[32,384]{1,0:T(8,128)} fusion(f32[7424,384]{1,0:T(8,128)} %slice.178), kind=kCustom, calls=%all-reduce-scatter | all-reduce-scatter fusion | flops 3145729 | bytes 11452416
  1347.8 16.5 %collective-permute-start.25 = (f32[32,384]{1,0:T(8,128)}, f32[32,384]{1,0:T(8,128)S(1)}, u32[]{:S(2)}, u32[]{:S(2)}) collective-permute-start(f32[32,384]{1,0:T(8,128)} %fusion), channel_id=1, source_target_pairs={{0,14},{1,15},{2,16},{3,17},{4,18},{5,19},{6,20},{7,21},{8,22},{9,... | collective-permute-start | bytes 147464
  1364.4 9.5 collective-permute-start.24
  1375.7 1.9 collective-permute-start.22
  1377.6 1.9 collective-permute-start.21
  1379.5 31.2 %collective-permute-start.20 = (f32[32,384]{1,0:T(8,128)}, f32[32,384]{1,0:T(8,128)S(1)}, u32[]{:S(2)}, u32[]{:S(2)}) collective-permute-start(f32[32,384]{1,0:T(8,128)} %fusion), channel_id=1, source_target_pairs={{0,9},{1,10},{2,11},{3,12},{4,13},{5,14},{6,15},{7,16},{8,17},{9,1... | collective-permute-start | bytes 147464
  1411.6 4.0 collective-permute-start.19
  1416.9 3.7 collective-permute-start.17
  1420.7 2.8 collective-permute-start.16
  1423.9 4.0 fusion.46
  1428.0 3.4 collective-permute-start.15
  1431.5 2.7 collective-permute-start.14
  1434.2 8.7 collective-permute-start.13
  1442.9 1.9 collective-permute-start.12
  1444.8 2.5 fusion.47
  1447.3 8.1 scatter_custom_fusion.3
  1455.5 7.6 scatter_custom_fusion.1
  1463.1 7.7 scatter_custom_fusion
  1472.3 9.4 scatter_custom_fusion.2
  1481.9 34.6 %concatenate.46 = f32[797,384]{1,0:T(8,128)} concatenate(f32[29,384]{1,0:T(8,128)S(1)} %copy-done.46, f32[32,384]{1,0:T(8,128)S(1)} %copy-done.42, f32[32,384]{1,0:T(8,128)S(1)} %copy-done.44, f32[32,384]{1,0:T(8,128)S(1)} %copy-done.48, f32[32,384]{1,0:T(8,128)S(1)} %copy-done.50, f32[32,384]{1,0:T(8,128)S(1)} %copy-done.52, f32[32,384]{1,0:T(8,128)S(1)} %copy-done.54, ...), dimensions={0} | concatenate | bytes 2448384
  1517.5 2.0 add_convert_fusion.2
  1521.6 36.5 %all-reduce.4.cloned.1.call-done = bf16[512,384]{1,0:T(8,128)(2,1)} async-done(((bf16[512,384]{1,0:T(8,128)(2,1)}), bf16[512,384]{1,0:T(8,128)(2,1)}) %all-reduce.4.cloned.1.call-update) | async-done | bytes 393232 | tf_op jit(solution)/shard_map/psum | solution.py:176
  1559.8 2.0 fusion.27
  (276 shorter events, 63.0 us)
Async XLA Ops:
  7.2 441.8 %all-gather.3.cloned.1.call-start = ((), (), s32[]{:S(2)}) async-start(), calls=%async_computation.1 | async-start | bytes 6316032 | tf_op jit(solution)/shard_map/all_gather | solution.py:106
  8.6 1549.5 %all-reduce.4.cloned.1.call-start = ((), (), s32[]{:S(2)}) async-start(), calls=%async_computation | async-start | bytes 786432 | tf_op jit(solution)/shard_map/psum | solution.py:176
  9.9 26.6 %collective-permute-start = (bf16[512,384]{1,0:T(8,128)(2,1)S(1)}, bf16[512,384]{1,0:T(8,128)(2,1)S(1)}, u32[]{:S(2)}, u32[]{:S(2)}) collective-permute-start(bf16[512,384]{1,0:T(8,128)(2,1)S(1)} %convert_element_type.90), channel_id=1, source_target_pairs={{0,4},{4,0},{8,12},{12,8},{16,20},{20,16},{24,28},{28,24},{32,36},... | collective-permute-start | bytes 1179656 | tf_op jit(solution)/shard_map/ppermute | solution.py:16
  36.6 22.1 %collective-permute-start.1 = (bf16[512,384]{1,0:T(8,128)(2,1)S(1)}, bf16[512,384]{1,0:T(8,128)(2,1)S(1)}, u32[]{:S(2)}, u32[]{:S(2)}) collective-permute-start(bf16[512,384]{1,0:T(8,128)(2,1)S(1)} %broadcast_select_fusion.5), channel_id=1, source_target_pairs={{0,8},{8,0},{4,12},{12,4},{16,24},{24,16},{20,28},{28,20},{32,40},... | collective-permute-start | bytes 1179656 | tf_op jit(solution)/shard_map/ppermute | solution.py:16
  58.7 23.7 %collective-permute-start.2 = (bf16[512,384]{1,0:T(8,128)(2,1)S(1)}, bf16[512,384]{1,0:T(8,128)(2,1)S(1)}, u32[]{:S(2)}, u32[]{:S(2)}) collective-permute-start(bf16[512,384]{1,0:T(8,128)(2,1)S(1)} %broadcast_select_fusion.6), channel_id=1, source_target_pairs={{0,16},{16,0},{4,20},{20,4},{8,24},{24,8},{12,28},{28,12},{32,48},... | collective-permute-start | bytes 1179656 | tf_op jit(solution)/shard_map/ppermute | solution.py:16
  82.5 11.1 collective-permute-start.3
  93.6 8.2 collective-permute-start.4
  101.9 9.0 collective-permute-start.5
  548.3 55.4 %copy-start.11 = (f32[1000,384]{1,0:T(8,128)S(1)}, f32[1000,384]{1,0:T(8,128)}, u32[]{:S(2)}) copy-start(f32[1000,384]{1,0:T(8,128)} %multiply_add_fusion) | copy-start | bytes 4608004
  549.9 7.6 collective-permute-start.6
  557.5 46.2 %copy-start.8 = (f32[1000,384]{1,0:T(8,128)S(1)}, f32[1000,384]{1,0:T(8,128)}, u32[]{:S(2)}) copy-start(f32[1000,384]{1,0:T(8,128)} %copy-done.7) | copy-start | bytes 4608004
  557.5 46.1 %copy-start.3 = (f32[1000,384]{1,0:T(8,128)S(1)}, f32[1000,384]{1,0:T(8,128)}, u32[]{:S(2)}) copy-start(f32[1000,384]{1,0:T(8,128)} %select_convert_fusion.1) | copy-start | bytes 4608004
  557.5 46.1 %copy-start.6 = (f32[1000,384]{1,0:T(8,128)S(1)}, f32[1000,384]{1,0:T(8,128)}, u32[]{:S(2)}) copy-start(f32[1000,384]{1,0:T(8,128)} %select_convert_fusion) | copy-start | bytes 4608004
  557.6 19.2 %collective-permute-start.7 = (bf16[512,384]{1,0:T(8,128)(2,1)S(1)}, bf16[512,384]{1,0:T(8,128)(2,1)S(1)}, u32[]{:S(2)}, u32[]{:S(2)}) collective-permute-start(bf16[512,384]{1,0:T(8,128)(2,1)S(1)} %fusion.31), channel_id=1, source_target_pairs={{0,8},{8,0},{4,12},{12,4},{16,24},{24,16},{20,28},{28,20},{32,40},... | collective-permute-start | bytes 1179656 | tf_op jit(solution)/shard_map/ppermute | solution.py:16
  576.9 21.9 %collective-permute-start.8 = (bf16[512,384]{1,0:T(8,128)(2,1)S(1)}, bf16[512,384]{1,0:T(8,128)(2,1)S(1)}, u32[]{:S(2)}, u32[]{:S(2)}) collective-permute-start(bf16[512,384]{1,0:T(8,128)(2,1)S(1)} %get-tuple-element.11), channel_id=1, source_target_pairs={{0,16},{16,0},{4,20},{20,4},{8,24},{24,8},{12,28},{28,12},{32,48},... | collective-permute-start | bytes 1179656 | tf_op jit(solution)/shard_map/ppermute | solution.py:16
  598.9 39.1 %collective-permute-start.9 = (bf16[512,384]{1,0:T(8,128)(2,1)S(1)}, bf16[512,384]{1,0:T(8,128)(2,1)}, u32[]{:S(2)}, u32[]{:S(2)}) collective-permute-start(bf16[512,384]{1,0:T(8,128)(2,1)S(1)} %fusion.32), channel_id=1, source_target_pairs={{0,32},{32,0},{4,36},{36,4},{8,40},{40,8},{12,44},{44,12},{16,48},... | collective-permute-start | bytes 1179656 | tf_op jit(solution)/shard_map/ppermute | solution.py:16
  639.1 740.4 %collective-permute-start.10 = (bf16[512,384]{1,0:T(8,128)(2,1)S(1)}, bf16[512,384]{1,0:T(8,128)(2,1)S(1)}, u32[]{:S(2)}, u32[]{:S(2)}) collective-permute-start(bf16[512,384]{1,0:T(8,128)(2,1)S(1)} %get-tuple-element.9), channel_id=1, source_target_pairs={{0,64},{64,0},{4,68},{68,4},{8,72},{72,8},{12,76},{76,12},{16,80},... | collective-permute-start | bytes 1179656 | tf_op jit(solution)/shard_map/ppermute | solution.py:16
  1333.5 90.3 %copy-start.38 = (bf16[1000,192]{1,0:T(8,128)(2,1)S(1)}, bf16[1000,192]{1,0:T(8,128)(2,1)}, u32[]{:S(2)}) copy-start(bf16[1000,192]{1,0:T(8,128)(2,1)} %copy-done.37) | copy-start | bytes 1152004
  1333.5 90.3 %copy-start.40 = (bf16[1000,192]{1,0:T(8,128)(2,1)S(1)}, bf16[1000,192]{1,0:T(8,128)(2,1)}, u32[]{:S(2)}) copy-start(bf16[1000,192]{1,0:T(8,128)(2,1)} %copy-done.39) | copy-start | bytes 1152004
  1333.5 7.7 collective-permute-start.34
  1335.0 7.6 collective-permute-start.33
  1337.1 2.8 collective-permute-start.35
  1338.4 5.5 collective-permute-start.32
  1339.9 88.0 %copy-start.45 = (f32[29,384]{1,0:T(8,128)}, f32[29,384]{1,0:T(8,128)S(1)}, u32[]{:S(2)}) copy-start(f32[29,384]{1,0:T(8,128)S(1)} %collective-permute-done.35) | copy-start | bytes 133636
  1339.9 5.2 collective-permute-start.31
  1341.2 86.7 %copy-start.41 = (f32[32,384]{1,0:T(8,128)}, f32[32,384]{1,0:T(8,128)S(1)}, u32[]{:S(2)}) copy-start(f32[32,384]{1,0:T(8,128)S(1)} %collective-permute-done.34) | copy-start | bytes 147460
  1341.2 5.3 collective-permute-start.30
  1342.5 85.4 %copy-start.43 = (f32[32,384]{1,0:T(8,128)}, f32[32,384]{1,0:T(8,128)S(1)}, u32[]{:S(2)}) copy-start(f32[32,384]{1,0:T(8,128)S(1)} %collective-permute-done.33) | copy-start | bytes 147460
  1342.5 5.3 collective-permute-start.29
  1343.8 84.1 %copy-start.47 = (f32[32,384]{1,0:T(8,128)}, f32[32,384]{1,0:T(8,128)S(1)}, u32[]{:S(2)}) copy-start(f32[32,384]{1,0:T(8,128)S(1)} %collective-permute-done.32) | copy-start | bytes 147460
  1343.9 20.5 %collective-permute-start.28 = (f32[32,384]{1,0:T(8,128)}, f32[32,384]{1,0:T(8,128)S(1)}, u32[]{:S(2)}, u32[]{:S(2)}) collective-permute-start(f32[32,384]{1,0:T(8,128)} %fusion), channel_id=1, source_target_pairs={{0,17},{1,18},{2,19},{3,20},{4,21},{5,22},{6,23},{7,24},{8,25},{9,... | collective-permute-start | bytes 147464
  1345.2 82.8 %copy-start.49 = (f32[32,384]{1,0:T(8,128)}, f32[32,384]{1,0:T(8,128)S(1)}, u32[]{:S(2)}) copy-start(f32[32,384]{1,0:T(8,128)S(1)} %collective-permute-done.31) | copy-start | bytes 147460
  1345.2 28.7 %collective-permute-start.27 = (f32[32,384]{1,0:T(8,128)}, f32[32,384]{1,0:T(8,128)S(1)}, u32[]{:S(2)}, u32[]{:S(2)}) collective-permute-start(f32[32,384]{1,0:T(8,128)} %fusion), channel_id=1, source_target_pairs={{0,16},{1,17},{2,18},{3,19},{4,20},{5,21},{6,22},{7,23},{8,24},{9,... | collective-permute-start | bytes 147464
  1346.5 81.4 %copy-start.51 = (f32[32,384]{1,0:T(8,128)}, f32[32,384]{1,0:T(8,128)S(1)}, u32[]{:S(2)}) copy-start(f32[32,384]{1,0:T(8,128)S(1)} %collective-permute-done.30) | copy-start | bytes 147460
  1346.5 29.2 %collective-permute-start.26 = (f32[32,384]{1,0:T(8,128)}, f32[32,384]{1,0:T(8,128)S(1)}, u32[]{:S(2)}, u32[]{:S(2)}) collective-permute-start(f32[32,384]{1,0:T(8,128)} %fusion), channel_id=1, source_target_pairs={{0,15},{1,16},{2,17},{3,18},{4,19},{5,20},{6,21},{7,22},{8,23},{9,... | collective-permute-start | bytes 147464
  1347.8 80.1 %copy-start.53 = (f32[32,384]{1,0:T(8,128)}, f32[32,384]{1,0:T(8,128)S(1)}, u32[]{:S(2)}) copy-start(f32[32,384]{1,0:T(8,128)S(1)} %collective-permute-done.29) | copy-start | bytes 147460
  1347.8 29.8 %collective-permute-start.25 = (f32[32,384]{1,0:T(8,128)}, f32[32,384]{1,0:T(8,128)S(1)}, u32[]{:S(2)}, u32[]{:S(2)}) collective-permute-start(f32[32,384]{1,0:T(8,128)} %fusion), channel_id=1, source_target_pairs={{0,14},{1,15},{2,16},{3,17},{4,18},{5,19},{6,20},{7,21},{8,22},{9,... | collective-permute-start | bytes 147464
  1364.4 63.6 %copy-start.55 = (f32[32,384]{1,0:T(8,128)}, f32[32,384]{1,0:T(8,128)S(1)}, u32[]{:S(2)}) copy-start(f32[32,384]{1,0:T(8,128)S(1)} %collective-permute-done.28) | copy-start | bytes 147460
  1364.4 47.2 %collective-permute-start.24 = (f32[32,384]{1,0:T(8,128)}, f32[32,384]{1,0:T(8,128)}, u32[]{:S(2)}, u32[]{:S(2)}) collective-permute-start(f32[32,384]{1,0:T(8,128)} %fusion), channel_id=1, source_target_pairs={{0,13},{1,14},{2,15},{3,16},{4,17},{5,18},{6,19},{7,20},{8,21},{9,... | collective-permute-start | bytes 147464
  1373.8 54.1 %copy-start.57 = (f32[32,384]{1,0:T(8,128)}, f32[32,384]{1,0:T(8,128)S(1)}, u32[]{:S(2)}) copy-start(f32[32,384]{1,0:T(8,128)S(1)} %collective-permute-done.27) | copy-start | bytes 147460
  1373.8 41.8 %collective-permute-start.23 = (f32[32,384]{1,0:T(8,128)}, f32[32,384]{1,0:T(8,128)}, u32[]{:S(2)}, u32[]{:S(2)}) collective-permute-start(f32[32,384]{1,0:T(8,128)} %fusion), channel_id=1, source_target_pairs={{0,12},{1,13},{2,14},{3,15},{4,16},{5,17},{6,18},{7,19},{8,20},{9,... | collective-permute-start | bytes 147464
  1375.7 52.2 %copy-start.59 = (f32[32,384]{1,0:T(8,128)}, f32[32,384]{1,0:T(8,128)S(1)}, u32[]{:S(2)}) copy-start(f32[32,384]{1,0:T(8,128)S(1)} %collective-permute-done.26) | copy-start | bytes 147460
  1375.7 41.2 %collective-permute-start.22 = (f32[32,384]{1,0:T(8,128)}, f32[32,384]{1,0:T(8,128)}, u32[]{:S(2)}, u32[]{:S(2)}) collective-permute-start(f32[32,384]{1,0:T(8,128)} %fusion), channel_id=1, source_target_pairs={{0,11},{1,12},{2,13},{3,14},{4,15},{5,16},{6,17},{7,18},{8,19},{9,... | collective-permute-start | bytes 147464
  1377.6 50.3 %copy-start.61 = (f32[32,384]{1,0:T(8,128)}, f32[32,384]{1,0:T(8,128)S(1)}, u32[]{:S(2)}) copy-start(f32[32,384]{1,0:T(8,128)S(1)} %collective-permute-done.25) | copy-start | bytes 147460
  1377.6 43.0 %collective-permute-start.21 = (f32[32,384]{1,0:T(8,128)}, f32[32,384]{1,0:T(8,128)}, u32[]{:S(2)}, u32[]{:S(2)}) collective-permute-start(f32[32,384]{1,0:T(8,128)} %fusion), channel_id=1, source_target_pairs={{0,10},{1,11},{2,12},{3,13},{4,14},{5,15},{6,16},{7,17},{8,18},{9,... | collective-permute-start | bytes 147464
  1379.5 48.5 %copy-start.27 = (bf16[512,384]{1,0:T(8,128)(2,1)}, bf16[512,384]{1,0:T(8,128)(2,1)S(1)}, u32[]{:S(2)}) copy-start(bf16[512,384]{1,0:T(8,128)(2,1)S(1)} %collective-permute-done.10) | copy-start | bytes 1179652
  1379.5 44.0 %collective-permute-start.20 = (f32[32,384]{1,0:T(8,128)}, f32[32,384]{1,0:T(8,128)S(1)}, u32[]{:S(2)}, u32[]{:S(2)}) collective-permute-start(f32[32,384]{1,0:T(8,128)} %fusion), channel_id=1, source_target_pairs={{0,9},{1,10},{2,11},{3,12},{4,13},{5,14},{6,15},{7,16},{8,17},{9,1... | collective-permute-start | bytes 147464
  1411.6 33.2 %copy-start.34 = (bf16[1000,192]{1,0:T(8,128)(2,1)S(1)}, bf16[1000,192]{1,0:T(8,128)(2,1)}, u32[]{:S(2)}) copy-start(bf16[1000,192]{1,0:T(8,128)(2,1)} %copy-done.33) | copy-start | bytes 1152004
  1411.6 33.2 %copy-start.36 = (bf16[1000,192]{1,0:T(8,128)(2,1)S(1)}, bf16[1000,192]{1,0:T(8,128)(2,1)}, u32[]{:S(2)}) copy-start(bf16[1000,192]{1,0:T(8,128)(2,1)} %copy-done.35) | copy-start | bytes 1152004
  1411.6 33.2 %copy-start.80 = (bf16[1000,1000]{1,0:T(8,128)(2,1)S(1)}, bf16[1000,1000]{1,0:T(8,128)(2,1)}, u32[]{:S(2)}) copy-start(bf16[1000,1000]{1,0:T(8,128)(2,1)} %copy-done.79) | copy-start | bytes 6000004
  1411.6 16.4 %collective-permute-start.19 = (f32[32,384]{1,0:T(8,128)}, f32[32,384]{1,0:T(8,128)S(1)}, u32[]{:S(2)}, u32[]{:S(2)}) collective-permute-start(f32[32,384]{1,0:T(8,128)} %fusion), channel_id=1, source_target_pairs={{0,8},{1,9},{2,10},{3,11},{4,12},{5,13},{6,14},{7,15},{8,16},{9,17... | collective-permute-start | bytes 147464
  1415.6 15.8 %collective-permute-start.18 = (f32[32,384]{1,0:T(8,128)}, f32[32,384]{1,0:T(8,128)S(1)}, u32[]{:S(2)}, u32[]{:S(2)}) collective-permute-start(f32[32,384]{1,0:T(8,128)} %fusion), channel_id=1, source_target_pairs={{0,7},{1,8},{2,9},{3,10},{4,11},{5,12},{6,13},{7,14},{8,15},{9,16}... | collective-permute-start | bytes 147464
  1416.9 17.3 %collective-permute-start.17 = (f32[32,384]{1,0:T(8,128)}, f32[32,384]{1,0:T(8,128)S(1)}, u32[]{:S(2)}, u32[]{:S(2)}) collective-permute-start(f32[32,384]{1,0:T(8,128)} %fusion), channel_id=1, source_target_pairs={{0,6},{1,7},{2,8},{3,9},{4,10},{5,11},{6,12},{7,13},{8,14},{9,15},... | collective-permute-start | bytes 147464
  1420.7 22.2 %collective-permute-start.16 = (f32[32,384]{1,0:T(8,128)}, f32[32,384]{1,0:T(8,128)S(1)}, u32[]{:S(2)}, u32[]{:S(2)}) collective-permute-start(f32[32,384]{1,0:T(8,128)} %fusion), channel_id=1, source_target_pairs={{0,5},{1,6},{2,7},{3,8},{4,9},{5,10},{6,11},{7,12},{8,13},{9,14},{... | collective-permute-start | bytes 147464
  1423.5 93.9 %collective-permute-start.11 = (bf16[512,384]{1,0:T(8,128)(2,1)}, bf16[512,384]{1,0:T(8,128)(2,1)}, u32[]{:S(2)}, u32[]{:S(2)}) collective-permute-start(bf16[512,384]{1,0:T(8,128)(2,1)} %fusion.33), channel_id=1, source_target_pairs={{0,128},{128,0},{4,132},{132,4},{8,136},{136,8},{12,140},{140,12},... | collective-permute-start | bytes 1179656 | tf_op jit(solution)/shard_map/ppermute | solution.py:16
  1428.0 53.7 %collective-permute-start.15 = (f32[32,384]{1,0:T(8,128)}, f32[32,384]{1,0:T(8,128)}, u32[]{:S(2)}, u32[]{:S(2)}) collective-permute-start(f32[32,384]{1,0:T(8,128)} %fusion), channel_id=1, source_target_pairs={{0,4},{1,5},{2,6},{3,7},{4,8},{5,9},{6,10},{7,11},{8,12},{9,13},{1... | collective-permute-start | bytes 147464
  1431.5 50.3 %collective-permute-start.14 = (f32[32,384]{1,0:T(8,128)}, f32[32,384]{1,0:T(8,128)}, u32[]{:S(2)}, u32[]{:S(2)}) collective-permute-start(f32[32,384]{1,0:T(8,128)} %fusion), channel_id=1, source_target_pairs={{0,3},{1,4},{2,5},{3,6},{4,7},{5,8},{6,9},{7,10},{8,11},{9,12},{10... | collective-permute-start | bytes 147464
  1434.2 47.5 %collective-permute-start.13 = (f32[32,384]{1,0:T(8,128)}, f32[32,384]{1,0:T(8,128)}, u32[]{:S(2)}, u32[]{:S(2)}) collective-permute-start(f32[32,384]{1,0:T(8,128)} %fusion), channel_id=1, source_target_pairs={{0,2},{1,3},{2,4},{3,5},{4,6},{5,7},{6,8},{7,9},{8,10},{9,11},{10,... | collective-permute-start | bytes 147464
  1442.9 38.9 %collective-permute-start.12 = (f32[32,384]{1,0:T(8,128)}, f32[32,384]{1,0:T(8,128)}, u32[]{:S(2)}, u32[]{:S(2)}) collective-permute-start(f32[32,384]{1,0:T(8,128)} %fusion), channel_id=1, source_target_pairs={{0,1},{1,2},{2,3},{3,4},{4,5},{5,6},{6,7},{7,8},{8,9},{9,10},{10,1... | collective-permute-start | bytes 147464
  1481.7 35.8 %copy-start.25 = (f32[512,384]{1,0:T(8,128)S(1)}, f32[512,384]{1,0:T(8,128)}, u32[]{:S(2)}) copy-start(f32[512,384]{1,0:T(8,128)} %scatter_custom_fusion.3) | copy-start | bytes 2359300
  1481.7 35.8 %copy-start.26 = (f32[512,384]{1,0:T(8,128)S(1)}, f32[512,384]{1,0:T(8,128)}, u32[]{:S(2)}) copy-start(f32[512,384]{1,0:T(8,128)} %scatter_custom_fusion.2) | copy-start | bytes 2359300
  1481.7 35.8 %copy-start.28 = (bf16[512,384]{1,0:T(8,128)(2,1)S(1)}, bf16[512,384]{1,0:T(8,128)(2,1)}, u32[]{:S(2)}) copy-start(bf16[512,384]{1,0:T(8,128)(2,1)} %copy-done.27) | copy-start | bytes 1179652
  1517.4 41.8 %copy-start.77 = (f32[512]{0:T(512)S(1)}, f32[512]{0:T(512)}, u32[]{:S(2)}) copy-start(f32[512]{0:T(512)} %param.14) | copy-start | bytes 6148
  1517.4 42.4 %copy-start.18 = (f32[512,384]{1,0:T(8,128)S(1)}, f32[512,384]{1,0:T(8,128)}, u32[]{:S(2)}) copy-start(f32[512,384]{1,0:T(8,128)} %param.13) | copy-start | bytes 2359300
  (56 other events, 374.9 us)
Sparse Core Ops, SparseCore 0:
  10.5 438.4 all-gather.2
  1519.6 38.4 all-reduce.3
where the time goes:
time: 1580 us; the launch traced here: 1570 us
  blocking collectives  694 us (44%)
  waiting for transfers between devices  455 us (29%)
  other arithmetic  134 us (8%)
  starting transfers between devices  131 us (8%)
  local copies, waits for them, and re-layouts  108 us (7%)
  matrix products  26.1 us (2%)
  between operations  20.4 us (1%)
    unnamed x1, blocking collectives  694 us
    all_gather x1, waiting for transfers between devices, fetch_relations(): whole_table = lax.all_gather(table_low, ('dom', 'rep'), axis=0, tiled=True)  317 us
    unnamed x24, starting transfers between devices  104 us
    ppermute x12, waiting for transfers between devices, swapped(): return lax.ppermute(block, axis, route)  101 us
    unnamed x167, local copies, waits for them, and re-layouts  50.9 us
    psum x1, waiting for transfers between devices, local(): lax.psum((head_sum + returned).astype(jnp.bfloat16), 'rep')  36.5 us
  transfers between devices with their start and end apart: 38, of which 11 were waited for; matrix products, arithmetic and copies ran while one was open for 54% of the time, Pallas kernels for 0%

commit v1 on v0

v1 whole, which is shorter than its diff:
```python
import functools

import jax
import jax.numpy as jnp
from jax import lax
from jax.experimental import pallas as pl
from jax.experimental.pallas import tpu as pltpu
from jax.sharding import PartitionSpec as P

LEARN = 0.1
NX, NY, NZ, NC = 4, 4, 8, 2
SIZES = {"x": NX, "y": NY, "z": NZ}
PARTS, HALF = 2, 16
SECOND, LAST = ("y", "x"), ("x", "y")
FOUR = 4
MESH = pl.DeviceIdType.MESH
VMEM_LIMIT = 56 * 1024 * 1024
CHUNK = FOUR * NZ * HALF
TILE = 512
LANES = 128
INNER = (((1,), (1,)), ((), ()))
FIRST = (((0,), (0,)), ((), ()))


def here():
    dom = lax.axis_index("dom")
    rep = lax.axis_index("rep")
    pos = {
        "y": dom // (2 * NZ),
        "x": lax.rem(dom // NZ, 2) * 2 + rep // 2,
        "z": lax.rem(dom, NZ),
    }
    return pos, lax.rem(rep, 2)


def device(pos, core):
    dom = pos["y"] * (2 * NZ) + (pos["x"] // 2) * NZ + pos["z"]
    rep = lax.rem(pos["x"], 2) * 2 + core
    return (dom, rep)


def moved(pos, axis, offset):
    there = dict(pos)
    there[axis] = lax.rem(pos[axis] + offset + SIZES[axis], SIZES[axis])
    return there


def beside(pos):
    there = dict(pos)
    there["x"] = pos["x"] + 1 - 2 * lax.rem(pos["x"], 2)
    return there


def greet(devices):
    barrier = pltpu.get_barrier_semaphore()
    for target in devices:
        pl.semaphore_signal(barrier, inc=1, device_id=target, device_id_type=MESH)
    pl.semaphore_wait(barrier, len(devices))


def all_peers(pos, core):
    peers = [device(pos, 1 - core)]
    for axis, count in SIZES.items():
        peers += [device(moved(pos, axis, step), core) for step in range(1, count)]
    return peers


class Copies:
    def __init__(self, send, recv):
        self.send, self.recv, self.started = send, recv, []

    def put(self, source, target, device_id):
        index = len(self.started)
        copy = pltpu.make_async_remote_copy(
            src_ref=source,
            dst_ref=target,
            send_sem=self.send.at[index],
            recv_sem=self.recv.at[index],
            device_id=device_id,
            device_id_type=MESH,
        )
        copy.start()
        self.started.append(copy)
        return copy

    def finish(self):
        for copy in self.started:
            copy.wait_send()


class Partner:
    ORDERS = (("x", "y", "z"), ("z", "y", "x"))
    COUNTS = {"x": 2, "y": NY, "z": NZ}

    def __init__(self, copies, pos, core, mask, buffers):
        self.copies, self.pos, self.core, self.buffers = copies, pos, core, buffers
        self.index = {"x": pos["x"] // 2, "y": pos["y"], "z": pos["z"]}
        self.bits = {"x": mask // NZ % 2, "y": mask // (2 * NZ), "z": mask % NZ}
        self.flying = {}

    def send(self, half, stage, rows):
        axis = self.ORDERS[half][stage]
        slots = self.buffers[half][axis]
        mine = slots.at[self.index[axis]]
        mine[...] = rows
        steps = (2,) if axis == "x" else range(1, self.COUNTS[axis])
        self.flying[half, stage] = [
            self.copies.put(mine, mine, device(moved(self.pos, axis, step), self.core))
            for step in steps
        ]

    def take(self, half, stage):
        axis = self.ORDERS[half][stage]
        for copy in self.flying[half, stage]:
            copy.wait_recv()
        return self.buffers[half][axis][jnp.bitwise_xor(self.index[axis], self.bits[axis])]

    @classmethod
    def scratch(cls, rows, width):
        return [
            pltpu.VMEM((cls.COUNTS[axis], rows, width), jnp.bfloat16)
            for _ in cls.ORDERS
            for axis in ("x", "y", "z")
        ]

    @staticmethod
    def name(refs):
        return [dict(zip(("x", "y", "z"), refs[:3])), dict(zip(("x", "y", "z"), refs[3:6]))]


def dot(a, b, dims=(((1,), (0,)), ((), ()))):
    return lax.dot_general(a, b, dims, preferred_element_type=jnp.float32)


def one_hot(ids, base, count):
    rows = lax.broadcasted_iota(jnp.int32, (count, ids.shape[1]), 0)
    return jnp.where(rows == ids - base, 1.0, 0.0).astype(jnp.bfloat16)


def at_part(part, first, second):
    return first + part * (second - first)


def chunk_base(part, core, second):
    return ((part * NC + core) * FOUR + second) * CHUNK


GATHER_COPIES = 80


def gather_kernel(
    plan_ref, ids_ref, rel_ref, own_ref, w_ref, partner_ref, table, w_sum, *rest
):
    buffers, (send, recv) = Partner.name(rest[:6]), rest[6:]
    pos, core = here()
    copies = Copies(send, recv)
    put = copies.put
    sibling = device(pos, 1 - core)
    x_low = lax.rem(pos["x"], 2)
    rows = partner_ref.shape[2]
    for part in range(PARTS):
        table[part, core, pos[SECOND[part]], pos[LAST[part]], pos["z"]] = rel_ref[part]
    w_sum[...] = jnp.zeros_like(w_sum)
    greet(all_peers(pos, core))

    along_z = []
    for part in range(PARTS):
        mine = table.at[part, core, pos[SECOND[part]], pos[LAST[part]], pos["z"]]
        along_z += [
            put(mine, mine, device(moved(pos, "z", step), core)) for step in range(1, NZ)
        ]
    partner = Partner(copies, pos, core, plan_ref[0], buffers)
    first = pl.multiple_of((x_low * NC + core) * rows, rows)
    partner.send(0, 0, own_ref[pl.ds(first, rows // 2), :])
    partner.send(1, 0, own_ref[pl.ds(first + rows // 2, rows // 2), :])

    along_second, along_last = [], []
    for copy in along_z:
        copy.wait_recv()

    def spread(part, step):
        where = moved(pos, SECOND[part], -step)
        column = table.at[part, core, where[SECOND[part]], pos[LAST[part]]]
        return [
            put(column, column, device(moved(pos, LAST[part], there), core))
            for there in range(1, FOUR)
        ]

    for part in range(PARTS):
        column = table.at[part, core, pos[SECOND[part]], pos[LAST[part]]]
        along_second.append(
            [
                put(column, column, device(moved(pos, SECOND[part], step), core))
                for step in range(1, FOUR)
            ]
        )
    along_last.append([spread(part, 0) for part in range(PARTS)])
    partner.send(0, 1, partner.take(0, 0))

    def add(which, step):
        @pl.loop(0, PARTS)
        def _(part):
            second = lax.rem(at_part(part, pos["y"], pos["x"]) - step + FOUR, FOUR)
            block = table[part, which, second].reshape(CHUNK, table.shape[-1])
            hot = one_hot(ids_ref[1:2, :], chunk_base(part, which, second), CHUNK)
            w_sum[...] += dot(block, hot, FIRST)

    across = []

    def cross(step):
        chunks = []
        for part in range(PARTS):
            for copy in along_last[step][part]:
                copy.wait_recv()
            second = moved(pos, SECOND[part], -step)[SECOND[part]]
            chunk = table.at[part, core, second]
            chunks.append(put(chunk, chunk, sibling))
        across.append(chunks)

    def add_across(step):
        for copy in across[step]:
            copy.wait_recv()
        add(1 - core, step)

    for step in range(1, FOUR):
        for part in range(PARTS):
            along_second[part][step - 1].wait_recv()
        along_last.append([spread(part, step) for part in range(PARTS)])
    partner.send(1, 1, partner.take(1, 0))
    cross(0)
    partner.send(0, 2, partner.take(0, 1))
    add(core, 0)
    cross(1)
    add_across(0)
    partner.send(1, 2, partner.take(1, 1))
    cross(2)
    add(core, 1)
    add_across(1)
    mine = partner_ref.at[x_low, core]
    other = partner_ref.at[1 - x_low, core]
    mine[: rows // 2, :] = partner.take(0, 2)
    mine[rows // 2 :, :] = partner.take(1, 2)
    to_side = put(mine, mine, device(beside(pos), core))
    to_sibling = put(mine, mine, sibling)
    cross(3)
    add(core, 2)
    to_side.wait_recv()
    last = put(other, other, sibling)
    add_across(2)
    add(core, 3)
    add_across(3)
    w_ref[...] = w_sum[...].astype(jnp.bfloat16)
    to_sibling.wait_recv()
    last.wait_recv()
    copies.finish()


def vmem_spec():
    return pl.BlockSpec(memory_space=pltpu.VMEM)


def smem_spec():
    return pl.BlockSpec(memory_space=pltpu.SMEM)


def gather_rows(plan, ids, rel, own):
    width = own.shape[1]
    lanes = ids.shape[1]
    rows = own.shape[0] // 4
    return pl.pallas_call(
        gather_kernel,
        out_shape=(
            jax.ShapeDtypeStruct((width, lanes), jnp.bfloat16),
            jax.ShapeDtypeStruct((2, NC, rows, width), jnp.bfloat16),
        ),
        in_specs=[smem_spec()] + [vmem_spec()] * 3,
        out_specs=(vmem_spec(),) * 2,
        scratch_shapes=[
            pltpu.VMEM((PARTS, NC, FOUR, FOUR, NZ, HALF, width), jnp.bfloat16),
            pltpu.VMEM((width, lanes), jnp.float32),
        ]
        + Partner.scratch(rows // 2, width)
        + [pltpu.SemaphoreType.DMA((GATHER_COPIES,))] * 2,
        compiler_params=pltpu.CompilerParams(
            collective_id=0, has_side_effects=True, vmem_limit_bytes=VMEM_LIMIT
        ),
    )(plan, ids, rel, own)


def compute_kernel(
    block_rows,
    samples,
    live_ref,
    ids_ref,
    negs_ref,
    own_ref,
    par_ref,
    w_ref,
    ent_ref,
    rg_ref,
    own_t,
    par_t,
    count_ref,
    head_acc,
    tail_acc,
):
    bf16 = jnp.bfloat16
    ent = own_ref.shape[0]
    half = own_ref.shape[1] // 2
    lanes = ids_ref.shape[1]
    own_t[...] = own_ref[...].astype(jnp.float32).T.astype(bf16)
    par_t[...] = par_ref[...].astype(jnp.float32).T.astype(bf16)
    ones = jnp.ones((negs_ref.shape[1], LANES), bf16)
    for row in range(4):
        count_ref[row] = dot(one_hot(negs_ref[row : row + 1, :], 0, ent), ones)
    head_acc[...] = jnp.zeros_like(head_acc)
    tail_acc[...] = jnp.zeros_like(tail_acc)

    @pl.loop(0, lanes // TILE)
    def _(tile):
        base = pl.multiple_of(tile * TILE, TILE)
        cols = pl.ds(base, TILE)
        slot = lax.broadcasted_iota(jnp.int32, (1, TILE), 1) + base
        act = jnp.where(slot < live_ref[0], 1.0, 0.0)
        in_first = slot < block_rows
        hot_h = one_hot(ids_ref[0:1, cols], 0, ent)
        hot_t = one_hot(ids_ref[2:3, cols], 0, ent)
        h = dot(own_t[...], hot_h)
        t = dot(par_t[...], hot_t)
        w = w_ref[:, cols].astype(jnp.float32)
        ha, hb, ta, tb, wa, wb = h[:half], h[half:], t[:half], t[half:], w[:half], w[half:]
        query = jnp.concatenate([ha * wa - hb * wb, ha * wb + hb * wa], axis=0)
        probe = jnp.concatenate([wa * ta + wb * tb, wa * tb - wb * ta], axis=0)
        positive = jnp.sum(query * t, axis=0, keepdims=True)
        query_low = query.astype(bf16)
        probe_low = probe.astype(bf16)
        pos_weight = -act * jax.nn.sigmoid(-positive)
        scaling = act / samples

        def weights(scores, row):
            repeats = TILE // LANES
            count = jnp.where(
                in_first,
                jnp.concatenate([count_ref[row]] * repeats, axis=1),
                jnp.concatenate([count_ref[row + 1]] * repeats, axis=1),
            )
            return (jax.nn.sigmoid(scores) * scaling * count).astype(bf16)

        tail_w = weights(dot(par_ref[...], query_low), 2)
        head_w = weights(dot(own_ref[...], probe_low), 0)
        qg = pos_weight * t + dot(par_t[...], tail_w)
        pg = dot(own_t[...], head_w)
        qa, qb, pa, pb = qg[:half], qg[half:], pg[:half], pg[half:]
        head_grad = jnp.concatenate([qa * wa + qb * wb, qb * wa - qa * wb], axis=0)
        tail_grad = (
            jnp.concatenate([pa * wa - pb * wb, pa * wb + pb * wa], axis=0) + pos_weight * query
        )
        rel_grad = jnp.concatenate(
            [qa * ha + qb * hb + pa * ta + pb * tb, qb * ha - qa * hb + pa * tb - pb * ta], axis=0
        )
        rg_ref[cols, :] = rel_grad.T.astype(bf16)
        head_acc[...] += dot(head_w, probe_low, INNER) + dot(hot_h, head_grad.astype(bf16), INNER)
        tail_acc[...] += dot(tail_w, query_low, INNER) + dot(hot_t, tail_grad.astype(bf16), INNER)

    shape = ent_ref.shape[1:]
    ent_ref[0] = head_acc[...].astype(bf16).reshape(shape)
    ent_ref[1] = tail_acc[...].astype(bf16).reshape(shape)


def compute(live, ids, negs, own, par, w, block_rows, samples):
    ent, width = own.shape
    lanes = ids.shape[1]
    return pl.pallas_call(
        functools.partial(compute_kernel, block_rows, samples),
        out_shape=(
            jax.ShapeDtypeStruct((2, 2, NC, ent // 4, width), jnp.bfloat16),
            jax.ShapeDtypeStruct((lanes, width), jnp.bfloat16),
        ),
        in_specs=[smem_spec()] + [vmem_spec()] * 5,
        out_specs=(vmem_spec(),) * 2,
        scratch_shapes=[
            pltpu.VMEM((width, ent), jnp.bfloat16),
            pltpu.VMEM((width, ent), jnp.bfloat16),
            pltpu.VMEM((4, ent, LANES), jnp.float32),
            pltpu.VMEM((ent, width), jnp.float32),
            pltpu.VMEM((ent, width), jnp.float32),
        ],
        compiler_params=pltpu.CompilerParams(vmem_limit_bytes=VMEM_LIMIT),
    )(live, ids, negs, own, par, w)


SCATTER_COPIES = 80


def scatter_kernel(
    plan_ref,
    ids_ref,
    rg_ref,
    ent_ref,
    rel_sum_ref,
    ent_sum_ref,
    for_core,
    from_core,
    product,
    total,
    in_last,
    two,
    in_second,
    three,
    in_z,
    ent_core,
    ent_half,
    ent_side,
    *rest,
):
    f32, bf16 = jnp.float32, jnp.bfloat16
    buffers, (send, recv) = Partner.name(rest[:6]), rest[6:]
    pos, core = here()
    copies = Copies(send, recv)
    put = copies.put
    sibling = device(pos, 1 - core)
    x_low = lax.rem(pos["x"], 2)
    rows = ent_ref.shape[3]
    width = ent_ref.shape[4]
    greet(all_peers(pos, core))
    ent_copy = put(ent_ref.at[:, :, 1 - core], ent_core, sibling)

    def chunk(part, which, step):
        second = lax.rem(at_part(part, pos["y"], pos["x"]) + step, FOUR)
        hot = one_hot(ids_ref[1:2, :], chunk_base(part, which, second), CHUNK)
        return dot(hot, rg_ref[...])

    def for_sibling(step):
        @pl.loop(0, PARTS)
        def _(part):
            for_core[step, part] = chunk(part, 1 - core, step).astype(bf16)

        return put(for_core.at[step], from_core.at[step], sibling)

    def for_chips(step, core_copy):
        @pl.loop(0, PARTS)
        def _(part):
            product[part] = chunk(part, core, step)

        core_copy.wait_recv()

        @pl.loop(0, PARTS)
        def _(part):
            summed = product[part] + from_core[step, part].astype(f32)
            total[step, part] = summed.astype(bf16).reshape(total.shape[2:])

        flying = []
        for part in range(PARTS):
            for there in range(1, FOUR):
                target = moved(pos, LAST[part], there)
                flying.append(
                    put(
                        total.at[step, part, target[LAST[part]]],
                        in_last.at[step, part, there - 1],
                        device(target, core),
                    )
                )
        return flying

    def sum_last(step, part):
        value = total[step, part, pos[LAST[part]]].astype(f32)
        for there in range(FOUR - 1):
            value += in_last[step, part, there].astype(f32)
        return value

    def to_second(step, flying):
        for copy in flying:
            copy.wait_recv()
        started = []
        for part in range(PARTS):
            two[step - 1, part] = sum_last(step, part).astype(bf16)
            started.append(
                put(
                    two.at[step - 1, part],
                    in_second.at[step - 1, part],
                    device(moved(pos, SECOND[part], step), core),
                )
            )
        return started

    partner = Partner(copies, pos, core, plan_ref[0], buffers)
    core_copy = for_sibling(1)
    ent_copy.wait_recv()
    ent_half[...] = (ent_ref[:, :, core].astype(f32) + ent_core[...].astype(f32)).astype(bf16)
    side_copy = put(ent_half.at[:, 1 - x_low], ent_side, device(beside(pos), core))
    flying_1 = for_chips(1, core_copy)
    core_copy = for_sibling(2)
    side_copy.wait_recv()
    piece = (ent_half[1, x_low].astype(f32) + ent_side[1].astype(f32)).astype(bf16)
    partner.send(1, 0, piece[rows // 2 :])
    partner.send(0, 0, piece[: rows // 2])
    flying_2 = for_chips(2, core_copy)
    seconds = to_second(1, flying_1)
    partner.send(0, 1, partner.take(0, 0))
    core_copy = for_sibling(3)
    flying_3 = for_chips(3, core_copy)
    partner.send(0, 2, partner.take(0, 1))
    seconds += to_second(2, flying_2)
    core_copy = for_sibling(0)
    partner.send(1, 1, partner.take(1, 0))
    flying_0 = for_chips(0, core_copy)
    partner.send(1, 2, partner.take(1, 1))
    seconds += to_second(3, flying_3)
    for copy in flying_0:
        copy.wait_recv()
    own = [sum_last(0, part) for part in range(PARTS)]
    for copy in seconds:
        copy.wait_recv()
    last_z = []
    for part in range(PARTS):
        value = own[part]
        for step in range(FOUR - 1):
            value += in_second[step, part].astype(f32)
        three[part] = value.astype(bf16)
        for step in range(1, NZ):
            target = moved(pos, "z", step)
            last_z.append(
                put(three.at[part, target["z"]], in_z.at[part, step - 1], device(target, core))
            )
    mine = ent_sum_ref.at[x_low, core]
    other = ent_sum_ref.at[1 - x_low, core]
    held = ent_half[0, x_low].astype(f32) + ent_side[0].astype(f32)
    for half in (1, 0):
        part_rows = slice(half * (rows // 2), (half + 1) * (rows // 2))
        mine[part_rows, :] = (held[part_rows] + partner.take(half, 2).astype(f32)).astype(bf16)
    to_side = put(mine, mine, device(beside(pos), core))
    to_sibling = put(mine, mine, sibling)
    to_side.wait_recv()
    last = put(other, other, sibling)
    for copy in last_z:
        copy.wait_recv()
    for part in range(PARTS):
        value = three[part, pos["z"]].astype(f32)
        for step in range(NZ - 1):
            value += in_z[part, step].astype(f32)
        rel_sum_ref[part] = value
    to_sibling.wait_recv()
    last.wait_recv()
    copies.finish()


def scatter_sums(plan, ids, rg, ent):
    rows, width = ent.shape[3:]
    bf16 = jnp.bfloat16
    column = (NZ, HALF, width)
    return pl.pallas_call(
        scatter_kernel,
        out_shape=(
            jax.ShapeDtypeStruct((PARTS, HALF, width), jnp.float32),
            jax.ShapeDtypeStruct((2, NC, rows, width), bf16),
        ),
        in_specs=[smem_spec()] + [vmem_spec()] * 3,
        out_specs=(vmem_spec(),) * 2,
        scratch_shapes=[
            pltpu.VMEM((FOUR, PARTS, CHUNK, width), bf16),
            pltpu.VMEM((FOUR, PARTS, CHUNK, width), bf16),
            pltpu.VMEM((PARTS, CHUNK, width), jnp.float32),
            pltpu.VMEM((FOUR, PARTS, FOUR) + column, bf16),
            pltpu.VMEM((FOUR, PARTS, FOUR - 1) + column, bf16),
            pltpu.VMEM((FOUR - 1, PARTS) + column, bf16),
            pltpu.VMEM((FOUR - 1, PARTS) + column, bf16),
            pltpu.VMEM((PARTS,) + column, bf16),
            pltpu.VMEM((PARTS, NZ - 1, HALF, width), bf16),
            pltpu.VMEM((2, 2, rows, width), bf16),
            pltpu.VMEM((2, 2, rows, width), bf16),
            pltpu.VMEM((2, rows, width), bf16),
        ]
        + Partner.scratch(rows // 2, width)
        + [pltpu.SemaphoreType.DMA((SCATTER_COPIES,))] * 2,
        compiler_params=pltpu.CompilerParams(
            collective_id=1, has_side_effects=True, vmem_limit_bytes=VMEM_LIMIT
        ),
    )(plan, ids, rg, ent)


def adagrad(param, state, grad):
    new_state = state + jnp.mean(grad * grad, axis=1)
    return (param - LEARN * grad / jnp.sqrt(new_state)[:, None], new_state)


def table_rows(ids, shard):
    owner, row = ids // shard, ids % shard
    dom, rep = owner // 4, owner % 4
    y, x, z = dom // (2 * NZ), (dom // NZ) % 2 * 2 + rep // 2, dom % NZ
    part = row // HALF
    second, last = at_part(part, y, x), at_part(part, x, y)
    return (((part * NC + rep % 2) * FOUR + second) * FOUR + last) * NZ * HALF + (
        z * HALF + row % HALF
    )


def local(
    entities,
    entity_state,
    relations,
    relation_state,
    head_ids,
    relation_ids,
    tail_ids,
    head_negatives,
    tail_negatives,
    bucket_sizes,
    plan,
):
    ent_rows, width = entities.shape
    shard = relations.shape[0]
    edge_slots = head_ids.shape[0]
    samples = head_negatives.shape[1]
    padded = -(-edge_slots // TILE) * TILE
    own_low = entities.astype(jnp.bfloat16)
    relation_low = jnp.pad(
        relations.astype(jnp.bfloat16), ((0, PARTS * HALF - shard), (0, 0))
    ).reshape(PARTS, HALF, width)
    ids = jnp.pad(
        jnp.stack([head_ids, table_rows(relation_ids, shard), tail_ids]),
        ((0, 0), (0, padded - edge_slots)),
        constant_values=-1,
    )
    live = jnp.minimum(bucket_sizes - lax.axis_index("rep") * edge_slots, edge_slots)
    negs = jnp.pad(
        jnp.concatenate([head_negatives, tail_negatives], axis=0),
        ((0, 0), (0, -samples % LANES)),
        constant_values=-1,
    )
    w, partner = gather_rows(plan, ids, relation_low, own_low)
    ent, rg = compute(
        live,
        ids,
        negs,
        own_low,
        partner.reshape(ent_rows, width),
        w,
        edge_slots // head_negatives.shape[0],
        samples,
    )
    relation_sum, summed = scatter_sums(plan, ids, rg, ent)
    summed = summed.reshape(ent_rows, width).astype(jnp.float32)
    new_entities, new_entity_state = adagrad(entities, entity_state, summed)
    relation_sum = relation_sum.reshape(PARTS * HALF, width)[:shard]
    new_relations, new_relation_state = adagrad(relations, relation_state, relation_sum)
    return (new_entities, new_entity_state, new_relations, new_relation_state)


def solution(mesh):
    placed = (
        P("dom", None),
        P("dom"),
        P(("dom", "rep"), None),
        P(("dom", "rep")),
        P(("dom", "rep")),
        P(("dom", "rep")),
        P(("dom", "rep")),
        P(("dom", "rep"), None),
        P(("dom", "rep"), None),
        P("dom"),
        P(),
    )
    return jax.shard_map(
        local,
        mesh=mesh,
        in_specs=placed,
        out_specs=(P("dom", None), P("dom"), P(("dom", "rep"), None), P(("dom", "rep"))),
        check_vma=False,
    )
```

time: 1580 us -> 145 us (0.09)
  blocking collectives: 694 us -> 0 us
  waiting for transfers between devices: 455 us -> 0 us
  Pallas kernels: 0 us -> 131 us
  starting transfers between devices: 131 us -> 0 us
  other arithmetic: 134 us -> 10.7 us
  local copies, waits for them, and re-layouts: 108 us -> 1.86 us
  matrix products: 26.1 us -> 0 us
  between operations: 20.4 us -> 1.34 us
    unnamed x1 -> x0, blocking collectives: 694 us -> none
    all_gather x1 -> x0, waiting for transfers between devices: 317 us -> none  [fetch_relations(): whole_table = lax.all_gather(table_low, ('dom', 'rep'), axis=0, tiled=True)]
    pallas_call x0 -> x3, Pallas kernels: none -> 131 us  [the longest x1 57.9 us: gather_rows(): pl.pallas_call(gather_kernel, out_shape=(jax.ShapeDtypeStruct((width, lan...]
    unnamed x24 -> x0, starting transfers between devices: 104 us -> none
    ppermute x12 -> x0, waiting for transfers between devices: 101 us -> none  [swapped(): return lax.ppermute(block, axis, route)]
    scatter-add x9 -> x0, other arithmetic: 89 us -> none  [the longest x1 20 us: ranged_sum(): summed = jax.ops.segment_sum(values, local_ids, num_segments=row_count + 1)]
    unnamed x167 -> x8, local copies, waits for them, and re-layouts: 50.9 us -> 0.02 us
    gather x9 -> x0, local copies, waits for them, and re-layouts: 47.5 us -> none  [the longest x1 10.8 us: fetch_relations(): return jnp.take(whole_table, relation_ids, axis=0)]
  transfers between devices with their start and end apart: 38 -> 0, of which waited for: 11 -> 0; matrix products, arithmetic and copies ran while one was open for 54% -> 0% of each run, Pallas kernels for 0% -> 0%
where the time goes in v1:
time: 145 us; the launch traced here: 144 us
  Pallas kernels  131 us (90%)
  other arithmetic  10.7 us (7%)
  local copies, waits for them, and re-layouts  1.86 us (1%)
    pallas_call x1, Pallas kernels, gather_rows(): pl.pallas_call(gather_kernel, out_shape=(jax.ShapeDtypeStruct((width, lan...  57.9 us
    pallas_call x1, Pallas kernels, scatter_sums(): pl.pallas_call(scatter_kernel, out_shape=(jax.ShapeDtypeStruct((PARTS, HA...  55 us
    pallas_call x1, Pallas kernels, compute(): pl.pallas_call(functools.partial(compute_kernel, block_rows, samples), ou...  17.8 us

profile of v1, /device:TPU:1, one launch (start us, length us, event | category | flops | bytes accessed | tf_op | source)
XLA Modules:
  0.0 144.5 jit_solution(5404717446517307575)
XLA Ops:
  1.3 0.8 fusion.8
  2.0 0.7 pad_add_fusion.1
  2.8 0.6 pad.13.negs_ref
  3.4 0.7 pad_add_fusion
  4.1 0.6 pad.12.ids_ref
  4.7 0.8 convert_element_type.14
  5.5 0.6 pad.14
  6.2 1.9 %convert_element_type.13.own_ref = bf16[512,384]{1,0:T(8,128)(2,1)} convert(f32[512,384]{1,0:T(8,128)} %param.11) | non-fusion elementwise | flops 196608 | bytes 1179648 | tf_op jit(solution)/shard_map/convert_element_type | solution.py:615
  8.1 57.9 %shard_map.138 = (bf16[384,2048]{1,0:T(8,128)(2,1)}, bf16[2,2,128,384]{3,2,1,0:T(8,128)(2,1)}) custom-call(s32[64]{0:T(128)} %plan_ref.3, s32[3,2048]{1,0:T(4,128)} %pad.12.ids_ref, bf16[2,16,384]{2,1,0:T(8,128)(2,1)} %bitcast.15, bf16[512,384]{1,0:T(8,128)(2,1)} %convert_element_type.13.own_ref), custom_call_target="tpu_custom_call" | custom-call | tf_op jit(solution)/shard_map/pallas_call | solution.py:270
  66.0 17.8 %shard_map.139 = (bf16[2,2,2,128,384]{4,3,2,1,0:T(8,128)(2,1)}, bf16[2048,384]{1,0:T(8,128)(2,1)}) custom-call(s32[1]{0:T(128)S(6)} %min.3.live_ref, s32[3,2048]{1,0:T(4,128)} %pad.12.ids_ref, s32[4,1024]{1,0:T(4,128)} %pad.13.negs_ref, bf16[512,384]{1,0:T(8,128)(2,1)} %convert_element_type.13.own_ref, bf16[512,384]{1,0:T(8,128)(2,1)} %bitcast.12, ...), custom_call_target="tpu_custom_call" | custom-call | tf_op jit(solution)/shard_map/pallas_call | solution.py:373
  83.8 0.0 copy-start.3
  83.8 0.0 copy-start.1
  83.8 0.0 copy-start.2
  83.8 0.0 copy-start
  83.8 55.0 %shard_map.140 = (f32[2,16,384]{2,1,0:T(8,128)}, bf16[2,2,128,384]{3,2,1,0:T(8,128)(2,1)}) custom-call(s32[64]{0:T(128)} %plan_ref.3, s32[3,2048]{1,0:T(4,128)} %pad.12.ids_ref, bf16[2048,384]{1,0:T(8,128)(2,1)} %get-tuple-element.12.rg_ref, bf16[2,2,2,128,384]{4,3,2,1,0:T(8,128)(2,1)} %get-tuple-element.13.ent_ref), custom_call_target="tpu_custom_call" | custom-call | tf_op jit(solution)/shard_map/pallas_call | solution.py:551
  138.8 0.9 multiply_reduce_fusion
  139.7 0.0 copy-done.3
  139.7 0.5 fusion.28
  140.2 0.0 copy-done.1
  140.2 1.5 %divide_subtract_fusion = f32[29,384]{1,0:T(8,128)} fusion(f32[29,384]{1,0:T(8,128)S(1)} %copy-done.1, f32[32,384]{1,0:T(8,128)} %bitcast.14, f32[29]{0:T(128)S(1)} %get-tuple-element.16), kind=kLoop, calls=%fused_computation.5 | loop fusion | flops 33408 | bytes 133748 | tf_op jit(solution)/shard_map/sub | solution.py:583
  141.7 1.2 fusion
  142.9 0.0 copy-done.2
  142.9 0.6 fusion.29
  143.5 0.0 copy-done
  143.5 1.0 fusion.1
  (1 shorter events, 0.0 us)
Async XLA Ops:
  83.8 55.9 %copy-start.3 = (f32[29]{0:T(128)S(1)}, f32[29]{0:T(128)}, u32[]{:S(2)}) copy-start(f32[29]{0:T(128)} %param.14) | copy-start | bytes 352
  83.8 56.4 %copy-start.1 = (f32[29,384]{1,0:T(8,128)S(1)}, f32[29,384]{1,0:T(8,128)}, u32[]{:S(2)}) copy-start(f32[29,384]{1,0:T(8,128)} %param.13) | copy-start | bytes 133636
  83.8 59.1 %copy-start.2 = (f32[512]{0:T(512)S(1)}, f32[512]{0:T(512)}, u32[]{:S(2)}) copy-start(f32[512]{0:T(512)} %param.12) | copy-start | bytes 6148
  83.8 59.7 %copy-start = (f32[512,384]{1,0:T(8,128)S(1)}, f32[512,384]{1,0:T(8,128)}, u32[]{:S(2)}) copy-start(f32[512,384]{1,0:T(8,128)} %param.11) | copy-start | bytes 2359300

commit v2 on v1

v2 whole, which is shorter than its diff:
```python
import functools

import jax
import jax.numpy as jnp
from jax import lax
from jax.experimental import pallas as pl
from jax.experimental.pallas import tpu as pltpu
from jax.sharding import PartitionSpec as P

LEARN = 0.1
NX, NY, NZ, NC = 4, 4, 8, 2
SIZES = {"x": NX, "y": NY, "z": NZ}
PARTS, HALF = 2, 16
SECOND, LAST = ("y", "x"), ("x", "y")
FOUR = 4
MESH = pl.DeviceIdType.MESH
VMEM_LIMIT = 56 * 1024 * 1024
CHUNK = FOUR * NZ * HALF
TILE = 512
LANES = 128
INNER = (((1,), (1,)), ((), ()))
FIRST = (((0,), (0,)), ((), ()))


def here():
    dom = lax.axis_index("dom")
    rep = lax.axis_index("rep")
    pos = {
        "y": dom // (2 * NZ),
        "x": lax.rem(dom // NZ, 2) * 2 + rep // 2,
        "z": lax.rem(dom, NZ),
    }
    return pos, lax.rem(rep, 2)


def device(pos, core):
    dom = pos["y"] * (2 * NZ) + (pos["x"] // 2) * NZ + pos["z"]
    rep = lax.rem(pos["x"], 2) * 2 + core
    return (dom, rep)


def moved(pos, axis, offset):
    there = dict(pos)
    there[axis] = lax.rem(pos[axis] + offset + SIZES[axis], SIZES[axis])
    return there


def beside(pos):
    there = dict(pos)
    there["x"] = pos["x"] + 1 - 2 * lax.rem(pos["x"], 2)
    return there


def signal_all(devices):
    barrier = pltpu.get_barrier_semaphore()
    for target in devices:
        pl.semaphore_signal(barrier, inc=1, device_id=target, device_id_type=MESH)


def wait_all(devices):
    pl.semaphore_wait(pltpu.get_barrier_semaphore(), len(devices))


def all_peers(pos, core):
    peers = [device(pos, 1 - core), device(beside(pos), 1 - core)]
    for axis, count in SIZES.items():
        peers += [device(moved(pos, axis, step), core) for step in range(1, count)]
    return peers


COPIES = 144


class Copies:
    def __init__(self, send, recv):
        self.send, self.recv, self.started = send, recv, []

    def put(self, source, target, device_id):
        index = len(self.started)
        assert index < COPIES
        copy = pltpu.make_async_remote_copy(
            src_ref=source,
            dst_ref=target,
            send_sem=self.send.at[index],
            recv_sem=self.recv.at[index],
            device_id=device_id,
            device_id_type=MESH,
        )
        copy.start()
        self.started.append(copy)
        return copy

    def finish(self):
        for copy in self.started:
            copy.wait_send()


class Partner:
    COUNTS = {"x": 2, "y": NY, "z_hi": NZ // 2, "z_lo": 2}

    def __init__(self, copies, pos, core, mask, refs):
        self.copies, self.pos, self.core = copies, pos, core
        names = list(self.COUNTS)
        self.buffers = [dict(zip(names, refs[:4])), dict(zip(names, refs[4:8]))]
        self.index = {
            "x": pos["x"] // 2,
            "y": pos["y"],
            "z_hi": pos["z"] // 2,
            "z_lo": lax.rem(pos["z"], 2),
        }
        self.bits = {
            "x": mask // NZ % 2,
            "y": mask // (2 * NZ),
            "z_hi": mask % NZ // 2,
            "z_lo": mask % 2,
        }
        self.flying = {}

    def peers(self, axis):
        pos = self.pos
        if axis == "x":
            return [moved(pos, "x", 2)]
        if axis == "y":
            return [moved(pos, "y", step) for step in range(1, NY)]
        if axis == "z_hi":
            return [moved(pos, "z", step) for step in range(2, NZ, 2)]
        return [moved(pos, "z", 1 - 2 * self.index["z_lo"])]

    def send(self, half, axis, rows):
        mine = self.buffers[half][axis].at[self.index[axis]]
        mine[...] = rows
        self.flying[half, axis] = [
            self.copies.put(mine, mine, device(there, self.core)) for there in self.peers(axis)
        ]

    def take(self, half, axis):
        for copy in self.flying[half, axis]:
            copy.wait_recv()
        return self.buffers[half][axis][jnp.bitwise_xor(self.index[axis], self.bits[axis])]

    def turn(self, axis, following):
        for half in range(2):
            self.send(half, following, self.take(half, axis))

    @classmethod
    def scratch(cls, rows, width):
        return [
            pltpu.VMEM((count, rows, width), jnp.bfloat16)
            for _ in range(2)
            for count in cls.COUNTS.values()
        ]


def to_replicas(put, whole, pos, core):
    mine = whole.at[lax.rem(pos["x"], 2), core]
    others = [device(beside(pos), core), device(beside(pos), 1 - core), device(pos, 1 - core)]
    return [put(mine, mine, target) for target in others]


def dot(a, b, dims=(((1,), (0,)), ((), ()))):
    return lax.dot_general(a, b, dims, preferred_element_type=jnp.float32)


def one_hot(ids, base, count):
    rows = lax.broadcasted_iota(jnp.int32, (count, ids.shape[1]), 0)
    return jnp.where(rows == ids - base, 1.0, 0.0).astype(jnp.bfloat16)


def at_part(part, first, second):
    return first + part * (second - first)


def chunk_base(part, core, second):
    return ((part * NC + core) * FOUR + second) * CHUNK


class Scratch:
    def __init__(self, ent, width, lanes, samples):
        rows = ent // 4
        bf16, f32 = jnp.bfloat16, jnp.float32
        column = (NZ, HALF, width)
        vmem = pltpu.VMEM
        self.shapes = {
            "ids": vmem((3, lanes), jnp.int32),
            "negs": vmem((4, -(-samples // LANES) * LANES), jnp.int32),
            "rel": vmem((PARTS * HALF, width), f32),
            "table": vmem((PARTS, NC, FOUR, FOUR) + column, bf16),
            "partner": vmem((2, NC, rows, width), bf16),
            "own": vmem((ent, width), bf16),
            "own_t": vmem((width, ent), bf16),
            "par_t": vmem((width, ent), bf16),
            "count": vmem((4, ent, LANES), f32),
            "h": vmem((width, lanes), bf16),
            "t": vmem((width, lanes), bf16),
            "w": vmem((width, lanes), f32),
            "head": vmem((ent, width), f32),
            "tail": vmem((ent, width), f32),
            "rg": vmem((lanes, width), bf16),
            "ent": vmem((2, 2, NC, rows, width), bf16),
            "for_core": vmem((FOUR, PARTS, CHUNK, width), bf16),
            "from_core": vmem((FOUR, PARTS, CHUNK, width), bf16),
            "product": vmem((PARTS, CHUNK, width), f32),
            "total": vmem((FOUR, PARTS, FOUR) + column, bf16),
            "in_last": vmem((FOUR, PARTS, FOUR - 1) + column, bf16),
            "two": vmem((FOUR - 1, PARTS) + column, bf16),
            "in_second": vmem((FOUR - 1, PARTS) + column, bf16),
            "three": vmem((PARTS,) + column, bf16),
            "in_z": vmem((PARTS, NZ - 1, HALF, width), bf16),
            "ent_core": vmem((2, 2, rows, width), bf16),
            "ent_half": vmem((2, 2, rows, width), bf16),
            "ent_side": vmem((2, rows, width), bf16),
            "send": pltpu.SemaphoreType.DMA((COPIES,)),
            "recv": pltpu.SemaphoreType.DMA((COPIES,)),
        }
        self.partner = Partner.scratch(rows // 2, width)

    def types(self):
        return list(self.shapes.values()) + self.partner + self.partner

    def bind(self, refs):
        for name, ref in zip(self.shapes, refs):
            setattr(self, name, ref)
        rest = refs[len(self.shapes) :]
        self.there, self.back = rest[:8], rest[8:]


def round_kernel(scratch, block_rows, samples, *refs):
    plan_ref, live_ref, ids_in, head_negs, tail_negs, rel_in, own_in = refs[:7]
    rel_sum_ref, ent_sum_ref = refs[7:9]
    v = scratch
    v.bind(refs[9:])
    f32, bf16 = jnp.float32, jnp.bfloat16
    pos, core = here()
    copies = Copies(v.send, v.recv)
    put = copies.put
    sibling = device(pos, 1 - core)
    x_low = lax.rem(pos["x"], 2)
    ent, width = own_in.shape
    half = width // 2
    rows = ent // 4
    lanes = v.w.shape[1]
    peers = all_peers(pos, core)

    signal_all(peers)
    shard = rel_in.shape[0]
    v.rel[...] = jnp.zeros_like(v.rel)
    v.rel[:shard, :] = rel_in[...]
    for part in range(PARTS):
        slot = v.table.at[part, core, pos[SECOND[part]], pos[LAST[part]], pos["z"]]
        slot[...] = v.rel[part * HALF : (part + 1) * HALF, :].astype(bf16)
    v.own[...] = own_in[...].astype(bf16)
    wait_all(peers)

    along_z = []
    for part in range(PARTS):
        mine = v.table.at[part, core, pos[SECOND[part]], pos[LAST[part]], pos["z"]]
        along_z += [
            put(mine, mine, device(moved(pos, "z", step), core)) for step in range(1, NZ)
        ]
    partner = Partner(copies, pos, core, plan_ref[0], v.there)
    first = pl.multiple_of((x_low * NC + core) * rows, rows)
    for side in range(2):
        partner.send(side, "x", v.own[pl.ds(first + side * (rows // 2), rows // 2), :])

    v.ids[...] = jnp.full_like(v.ids, -1)
    v.ids[:, : ids_in.shape[1]] = ids_in[...]
    v.negs[...] = jnp.full_like(v.negs, -1)
    v.negs[0:2, :samples] = head_negs[...]
    v.negs[2:4, :samples] = tail_negs[...]
    v.own_t[...] = v.own[...].astype(f32).T.astype(bf16)
    v.w[...] = jnp.zeros_like(v.w)
    v.head[...] = jnp.zeros_like(v.head)
    v.tail[...] = jnp.zeros_like(v.tail)
    partner.turn("x", "y")
    for copy in along_z:
        copy.wait_recv()

    along_second, along_last = [], []

    def spread(part, step):
        where = moved(pos, SECOND[part], -step)
        column = v.table.at[part, core, where[SECOND[part]], pos[LAST[part]]]
        return [
            put(column, column, device(moved(pos, LAST[part], there), core))
            for there in range(1, FOUR)
        ]

    for part in range(PARTS):
        column = v.table.at[part, core, pos[SECOND[part]], pos[LAST[part]]]
        along_second.append(
            [
                put(column, column, device(moved(pos, SECOND[part], step), core))
                for step in range(1, FOUR)
            ]
        )
    along_last.append([spread(part, 0) for part in range(PARTS)])
    partner.turn("y", "z_hi")
    for step in range(1, FOUR):
        for part in range(PARTS):
            along_second[part][step - 1].wait_recv()
        along_last.append([spread(part, step) for part in range(PARTS)])

    def tiles(body):
        @pl.loop(0, lanes // TILE)
        def _(tile):
            base = pl.multiple_of(tile * TILE, TILE)
            body(base, pl.ds(base, TILE))

    def gather_heads(base, cols):
        v.h[:, cols] = dot(v.own_t[...], one_hot(v.ids[0:1, cols], 0, ent)).astype(bf16)

    def gather_tails(base, cols):
        v.t[:, cols] = dot(v.par_t[...], one_hot(v.ids[2:3, cols], 0, ent)).astype(bf16)

    def add(which, step):
        @pl.loop(0, PARTS)
        def _(part):
            second = lax.rem(at_part(part, pos["y"], pos["x"]) - step + FOUR, FOUR)
            block = v.table[part, which, second].reshape(CHUNK, width)
            hot = one_hot(v.ids[1:2, :], chunk_base(part, which, second), CHUNK)
            v.w[...] += dot(block, hot, FIRST)

    across = []

    def cross(step):
        chunks = []
        for part in range(PARTS):
            for copy in along_last[step][part]:
                copy.wait_recv()
            second = moved(pos, SECOND[part], -step)[SECOND[part]]
            chunk = v.table.at[part, core, second]
            chunks.append(put(chunk, chunk, sibling))
        across.append(chunks)

    def add_across(step):
        for copy in across[step]:
            copy.wait_recv()
        add(1 - core, step)

    tiles(gather_heads)
    ones = jnp.ones((v.negs.shape[1], LANES), bf16)
    for row in range(4):
        v.count[row] = dot(one_hot(v.negs[row : row + 1, :], 0, ent), ones)
    cross(0)
    partner.turn("z_hi", "z_lo")
    add(core, 0)
    cross(1)
    mine = v.partner.at[x_low, core]
    mine[: rows // 2, :] = partner.take(0, "z_lo")
    mine[rows // 2 :, :] = partner.take(1, "z_lo")
    replicas = to_replicas(put, v.partner, pos, core)
    add_across(0)
    cross(2)
    add(core, 1)
    add_across(1)
    cross(3)
    add(core, 2)
    for copy in replicas:
        copy.wait_recv()
    v.par_t[...] = v.partner[...].reshape(ent, width).astype(f32).T.astype(bf16)
    tiles(gather_tails)
    add_across(2)
    add(core, 3)
    add_across(3)

    def edges(base, cols):
        slot = lax.broadcasted_iota(jnp.int32, (1, TILE), 1) + base
        act = jnp.where(slot < live_ref[0], 1.0, 0.0)
        in_first = slot < block_rows
        par = v.partner[...].reshape(ent, width)
        h, t, w = v.h[:, cols].astype(f32), v.t[:, cols].astype(f32), v.w[:, cols]
        ha, hb, ta, tb, wa, wb = h[:half], h[half:], t[:half], t[half:], w[:half], w[half:]
        query = jnp.concatenate([ha * wa - hb * wb, ha * wb + hb * wa], axis=0)
        probe = jnp.concatenate([wa * ta + wb * tb, wa * tb - wb * ta], axis=0)
        positive = jnp.sum(query * t, axis=0, keepdims=True)
        query_low = query.astype(bf16)
        probe_low = probe.astype(bf16)
        pos_weight = -act * jax.nn.sigmoid(-positive)
        scaling = act / samples

        def weights(scores, row):
            repeats = TILE // LANES
            count = jnp.where(
                in_first,
                jnp.concatenate([v.count[row]] * repeats, axis=1),
                jnp.concatenate([v.count[row + 1]] * repeats, axis=1),
            )
            return (jax.nn.sigmoid(scores) * scaling * count).astype(bf16)

        tail_w = weights(dot(par, query_low), 2)
        head_w = weights(dot(v.own[...], probe_low), 0)
        qg = pos_weight * t + dot(v.par_t[...], tail_w)
        pg = dot(v.own_t[...], head_w)
        qa, qb, pa, pb = qg[:half], qg[half:], pg[:half], pg[half:]
        head_grad = jnp.concatenate([qa * wa + qb * wb, qb * wa - qa * wb], axis=0)
        tail_grad = (
            jnp.concatenate([pa * wa - pb * wb, pa * wb + pb * wa], axis=0) + pos_weight * query
        )
        rel_grad = jnp.concatenate(
            [qa * ha + qb * hb + pa * ta + pb * tb, qb * ha - qa * hb + pa * tb - pb * ta], axis=0
        )
        v.rg[cols, :] = rel_grad.T.astype(bf16)
        hot_h = one_hot(v.ids[0:1, cols], 0, ent)
        hot_t = one_hot(v.ids[2:3, cols], 0, ent)
        v.head[...] += dot(head_w, probe_low, INNER) + dot(hot_h, head_grad.astype(bf16), INNER)
        v.tail[...] += dot(tail_w, query_low, INNER) + dot(hot_t, tail_grad.astype(bf16), INNER)

    tiles(edges)
    shape = v.ent.shape[1:]
    v.ent[0] = v.head[...].astype(bf16).reshape(shape)
    v.ent[1] = v.tail[...].astype(bf16).reshape(shape)

    ent_copy = put(v.ent.at[:, :, 1 - core], v.ent_core, sibling)

    def chunk(part, which, step):
        second = lax.rem(at_part(part, pos["y"], pos["x"]) + step, FOUR)
        hot = one_hot(v.ids[1:2, :], chunk_base(part, which, second), CHUNK)
        return dot(hot, v.rg[...])

    def for_sibling(step):
        @pl.loop(0, PARTS)
        def _(part):
            v.for_core[step, part] = chunk(part, 1 - core, step).astype(bf16)

        return put(v.for_core.at[step], v.from_core.at[step], sibling)

    def for_chips(step, core_copy):
        @pl.loop(0, PARTS)
        def _(part):
            v.product[part] = chunk(part, core, step)

        core_copy.wait_recv()

        @pl.loop(0, PARTS)
        def _(part):
            summed = v.product[part] + v.from_core[step, part].astype(f32)
            v.total[step, part] = summed.astype(bf16).reshape(v.total.shape[2:])

        flying = []
        for part in range(PARTS):
            for there in range(1, FOUR):
                target = moved(pos, LAST[part], there)
                flying.append(
                    put(
                        v.total.at[step, part, target[LAST[part]]],
                        v.in_last.at[step, part, there - 1],
                        device(target, core),
                    )
                )
        return flying

    def sum_last(step, part):
        value = v.total[step, part, pos[LAST[part]]].astype(f32)
        for there in range(FOUR - 1):
            value += v.in_last[step, part, there].astype(f32)
        return value

    def to_second(step, flying):
        for copy in flying:
            copy.wait_recv()
        started = []
        for part in range(PARTS):
            v.two[step - 1, part] = sum_last(step, part).astype(bf16)
            started.append(
                put(
                    v.two.at[step - 1, part],
                    v.in_second.at[step - 1, part],
                    device(moved(pos, SECOND[part], step), core),
                )
            )
        return started

    partner = Partner(copies, pos, core, plan_ref[0], v.back)
    core_copy = for_sibling(1)
    ent_copy.wait_recv()
    v.ent_half[...] = (v.ent[:, :, core].astype(f32) + v.ent_core[...].astype(f32)).astype(bf16)
    side_copy = put(v.ent_half.at[:, 1 - x_low], v.ent_side, device(beside(pos), core))
    flying_1 = for_chips(1, core_copy)
    core_copy = for_sibling(2)
    side_copy.wait_recv()
    piece = (v.ent_half[1, x_low].astype(f32) + v.ent_side[1].astype(f32)).astype(bf16)
    partner.send(0, "z_hi", piece[: rows // 2])
    partner.send(1, "z_hi", piece[rows // 2 :])
    flying_2 = for_chips(2, core_copy)
    seconds = to_second(1, flying_1)
    core_copy = for_sibling(3)
    partner.turn("z_hi", "z_lo")
    flying_3 = for_chips(3, core_copy)
    seconds += to_second(2, flying_2)
    partner.turn("z_lo", "y")
    core_copy = for_sibling(0)
    flying_0 = for_chips(0, core_copy)
    partner.turn("y", "x")
    seconds += to_second(3, flying_3)
    for copy in flying_0:
        copy.wait_recv()
    own = [sum_last(0, part) for part in range(PARTS)]
    for copy in seconds:
        copy.wait_recv()
    last_z = []
    for part in range(PARTS):
        value = own[part]
        for step in range(FOUR - 1):
            value += v.in_second[step, part].astype(f32)
        v.three[part] = value.astype(bf16)
        for step in range(1, NZ):
            target = moved(pos, "z", step)
            last_z.append(
                put(
                    v.three.at[part, target["z"]],
                    v.in_z.at[part, step - 1],
                    device(target, core),
                )
            )
    mine = ent_sum_ref.at[x_low, core]
    held = v.ent_half[0, x_low].astype(f32) + v.ent_side[0].astype(f32)
    for side in range(2):
        some = slice(side * (rows // 2), (side + 1) * (rows // 2))
        mine[some, :] = (held[some] + partner.take(side, "x").astype(f32)).astype(bf16)
    replicas = to_replicas(put, ent_sum_ref, pos, core)
    for copy in last_z:
        copy.wait_recv()
    for part in range(PARTS):
        value = v.three[part, pos["z"]].astype(f32)
        for step in range(NZ - 1):
            value += v.in_z[part, step].astype(f32)
        rel_sum_ref[part] = value
    for copy in replicas:
        copy.wait_recv()
    copies.finish()


def whole_round(plan, live, ids, head_negs, tail_negs, rel, own, block_rows):
    ent, width = own.shape
    samples = head_negs.shape[1]
    lanes = -(-ids.shape[1] // TILE) * TILE
    scratch = Scratch(ent, width, lanes, samples)
    smem = pl.BlockSpec(memory_space=pltpu.SMEM)
    vmem = pl.BlockSpec(memory_space=pltpu.VMEM)
    return pl.pallas_call(
        functools.partial(round_kernel, scratch, block_rows, samples),
        out_shape=(
            jax.ShapeDtypeStruct((PARTS, HALF, width), jnp.float32),
            jax.ShapeDtypeStruct((2, NC, ent // 4, width), jnp.bfloat16),
        ),
        in_specs=[smem] * 2 + [vmem] * 5,
        out_specs=(vmem,) * 2,
        scratch_shapes=scratch.types(),
        compiler_params=pltpu.CompilerParams(
            collective_id=0, has_side_effects=True, vmem_limit_bytes=VMEM_LIMIT
        ),
    )(plan, live, ids, head_negs, tail_negs, rel, own)


def adagrad(param, state, grad):
    new_state = state + jnp.mean(grad * grad, axis=1)
    return (param - LEARN * grad / jnp.sqrt(new_state)[:, None], new_state)


def table_rows(ids, shard):
    owner, row = ids // shard, ids % shard
    dom, rep = owner // 4, owner % 4
    y, x, z = dom // (2 * NZ), (dom // NZ) % 2 * 2 + rep // 2, dom % NZ
    part = row // HALF
    second, last = at_part(part, y, x), at_part(part, x, y)
    return (((part * NC + rep % 2) * FOUR + second) * FOUR + last) * NZ * HALF + (
        z * HALF + row % HALF
    )


def local(
    entities,
    entity_state,
    relations,
    relation_state,
    head_ids,
    relation_ids,
    tail_ids,
    head_negatives,
    tail_negatives,
    bucket_sizes,
    plan,
):
    ent_rows, width = entities.shape
    shard = relations.shape[0]
    edge_slots = head_ids.shape[0]
    ids = jnp.stack([head_ids, table_rows(relation_ids, shard), tail_ids])
    live = jnp.minimum(bucket_sizes - lax.axis_index("rep") * edge_slots, edge_slots)
    relation_sum, summed = whole_round(
        plan,
        live,
        ids,
        head_negatives,
        tail_negatives,
        relations,
        entities,
        edge_slots // head_negatives.shape[0],
    )
    summed = summed.reshape(ent_rows, width).astype(jnp.float32)
    new_entities, new_entity_state = adagrad(entities, entity_state, summed)
    relation_sum = relation_sum.reshape(PARTS * HALF, width)[:shard]
    new_relations, new_relation_state = adagrad(relations, relation_state, relation_sum)
    return (new_entities, new_entity_state, new_relations, new_relation_state)


def solution(mesh):
    placed = (
        P("dom", None),
        P("dom"),
        P(("dom", "rep"), None),
        P(("dom", "rep")),
        P(("dom", "rep")),
        P(("dom", "rep")),
        P(("dom", "rep")),
        P(("dom", "rep"), None),
        P(("dom", "rep"), None),
        P("dom"),
        P(),
    )
    return jax.shard_map(
        local,
        mesh=mesh,
        in_specs=placed,
        out_specs=(P("dom", None), P("dom"), P(("dom", "rep"), None), P(("dom", "rep"))),
        check_vma=False,
    )
```

time: 145 us -> 123 us (0.85)
  Pallas kernels: 131 us -> 114 us
  other arithmetic: 10.7 us -> 5.59 us
    pallas_call x3 -> x1, Pallas kernels: 131 us -> 114 us  [whole_round(): pl.pallas_call(functools.partial(round_kernel, scratch, block_rows, sampl...]
    convert_element_type x2 -> x0, other arithmetic: 2.73 us -> none  [the longest x1 1.92 us: local(): own_low = entities.astype(jnp.bfloat16)]
    pad x3 -> x0, local copies, waits for them, and re-layouts: 1.84 us -> none  [the longest x1 0.62 us: local(): jnp.pad(jnp.stack([head_ids, table_rows(relation_ids, shard), tail_ids]),...]
where the time goes in v2:
time: 123 us; the launch traced here: 122 us
  Pallas kernels  114 us (93%)
  other arithmetic  5.59 us (5%)
  between operations  1.35 us (1%)
  local copies, waits for them, and re-layouts  1.24 us (1%)
    pallas_call x1, Pallas kernels, whole_round(): pl.pallas_call(functools.partial(round_kernel, scratch, block_rows, sampl...  114 us

profile of v2, /device:TPU:1, one launch (start us, length us, event | category | flops | bytes accessed | tf_op | source)
XLA Modules:
  0.0 122.4 jit_solution(2025231539234105465)
XLA Ops:
  0.6 0.0 copy-start.4
  0.6 0.0 copy-start.3
  0.7 0.8 fusion.8
  1.4 0.0 copy-done.4
  1.4 0.0 copy-done.3
  1.4 0.6 pad_add_fusion.refs_2_
  2.7 114.3 %shard_map.138 = (f32[2,16,384]{2,1,0:T(8,128)}, bf16[2,2,128,384]{3,2,1,0:T(8,128)(2,1)}) custom-call(s32[64]{0:T(128)} %refs_0_.1, s32[1]{0:T(128)S(6)} %min.3.refs_1_, s32[3,2000]{1,0:T(4,128)} %pad_add_fusion.refs_2_, s32[2,1000]{1,0:T(2,128)} %refs_3_.1, s32[2,1000]{1,0:T(2,128)} %refs_4_.1, f32[29,384]{1,0:T(8,128)} %refs_5_.1, f32[512,384]{1,0:T(8,128)} %refs_6_.1), custom_call_target="tpu_custom_call" | custom-call | tf_op jit(solution)/shard_map/pallas_call | solution.py:540
  117.0 0.0 copy-start
  117.0 1.2 %fusion = (f32[2,2,128]{2,1,0:T(2,128)S(1)}, f32[2,2,128,384]{3,2,1,0:T(8,128)S(1)}) fusion(bf16[2,2,128,384]{3,2,1,0:T(8,128)(2,1)} %get-tuple-element.6), kind=kLoop, calls=%fused_computation.2 | loop fusion | flops 785920 | bytes 1181696 | tf_op jit(solution)/shard_map/reduce_sum | solution.py:556
  118.3 0.0 copy-start.5
  118.3 0.7 copy-done.5
  118.9 0.6 fusion.29
  119.5 0.0 copy-done
  119.5 0.0 copy-start.1
  119.5 1.0 fusion.1
  120.6 0.0 copy-start.2
  120.6 0.0 copy-done.1
  120.6 0.0 copy-start.6
  120.6 0.1 multiply_reduce_fusion
  120.7 0.6 copy-done.6
  121.2 0.5 fusion.28
  121.7 0.0 copy-done.2
  121.7 0.7 divide_subtract_fusion
  (1 shorter events, 0.0 us)
Async XLA Ops:
  0.6 0.8 copy-start.4
  0.6 0.8 copy-start.3
  117.0 2.5 %copy-start = (f32[512,384]{1,0:T(8,128)S(1)}, f32[512,384]{1,0:T(8,128)}, u32[]{:S(2)}) copy-start(f32[512,384]{1,0:T(8,128)} %refs_6_.1) | copy-start | bytes 2359300
  118.3 0.7 copy-start.5
  119.5 1.0 copy-start.1
  120.6 1.2 copy-start.2
  120.6 0.7 copy-start.6

commit v3 on v2

--- a/solution.py
+++ b/solution.py
@@ -15,7 +15,8 @@
 FOUR = 4
 MESH = pl.DeviceIdType.MESH
 VMEM_LIMIT = 56 * 1024 * 1024
-CHUNK = FOUR * NZ * HALF
+COLUMN = NZ * HALF
+CHUNK = FOUR * COLUMN
 TILE = 512
 LANES = 128
 INNER = (((1,), (1,)), ((), ()))
@@ -68,7 +69,7 @@
     return peers
 
 
-COPIES = 144
+COPIES = 176
 
 
 class Copies:
@@ -179,6 +180,7 @@
         rows = ent // 4
         bf16, f32 = jnp.bfloat16, jnp.float32
         column = (NZ, HALF, width)
+        turned = (width, COLUMN)
         vmem = pltpu.VMEM
         self.shapes = {
             "ids": vmem((3, lanes), jnp.int32),
@@ -193,17 +195,17 @@
             "h": vmem((width, lanes), bf16),
             "t": vmem((width, lanes), bf16),
             "w": vmem((width, lanes), f32),
-            "head": vmem((ent, width), f32),
-            "tail": vmem((ent, width), f32),
-            "rg": vmem((lanes, width), bf16),
+            "head": vmem((width, ent), f32),
+            "tail": vmem((width, ent), f32),
+            "rg": vmem((width, lanes), bf16),
             "ent": vmem((2, 2, NC, rows, width), bf16),
-            "for_core": vmem((FOUR, PARTS, CHUNK, width), bf16),
-            "from_core": vmem((FOUR, PARTS, CHUNK, width), bf16),
-            "product": vmem((PARTS, CHUNK, width), f32),
-            "total": vmem((FOUR, PARTS, FOUR) + column, bf16),
-            "in_last": vmem((FOUR, PARTS, FOUR - 1) + column, bf16),
-            "two": vmem((FOUR - 1, PARTS) + column, bf16),
-            "in_second": vmem((FOUR - 1, PARTS) + column, bf16),
+            "for_core": vmem((FOUR, PARTS * FOUR) + turned, bf16),
+            "from_core": vmem((FOUR, PARTS * FOUR) + turned, bf16),
+            "product": vmem((PARTS * FOUR,) + turned, f32),
+            "total": vmem((FOUR, PARTS * FOUR) + turned, bf16),
+            "in_last": vmem((FOUR, PARTS, FOUR - 1) + turned, bf16),
+            "two": vmem((FOUR - 1, PARTS) + turned, bf16),
+            "in_second": vmem((FOUR - 1, PARTS) + turned, bf16),
             "three": vmem((PARTS,) + column, bf16),
             "in_z": vmem((PARTS, NZ - 1, HALF, width), bf16),
             "ent_core": vmem((2, 2, rows, width), bf16),
@@ -271,6 +273,23 @@
     v.w[...] = jnp.zeros_like(v.w)
     v.head[...] = jnp.zeros_like(v.head)
     v.tail[...] = jnp.zeros_like(v.tail)
+
+    def tiles(body):
+        @pl.loop(0, lanes // TILE)
+        def _(tile):
+            base = pl.multiple_of(tile * TILE, TILE)
+            body(base, pl.ds(base, TILE))
+
+    def gather_heads(base, cols):
+        v.h[:, cols] = dot(v.own_t[...], one_hot(v.ids[0:1, cols], 0, ent)).astype(bf16)
+
+    def gather_tails(base, cols):
+        v.t[:, cols] = dot(v.par_t[...], one_hot(v.ids[2:3, cols], 0, ent)).astype(bf16)
+
+    tiles(gather_heads)
+    ones = jnp.ones((v.negs.shape[1], LANES), bf16)
+    for row in range(4):
+        v.count[row] = dot(one_hot(v.negs[row : row + 1, :], 0, ent), ones)
     partner.turn("x", "y")
     for copy in along_z:
         copy.wait_recv()
@@ -300,68 +319,81 @@
             along_second[part][step - 1].wait_recv()
         along_last.append([spread(part, step) for part in range(PARTS)])
 
-    def tiles(body):
-        @pl.loop(0, lanes // TILE)
-        def _(tile):
-            base = pl.multiple_of(tile * TILE, TILE)
-            body(base, pl.ds(base, TILE))
-
-    def gather_heads(base, cols):
-        v.h[:, cols] = dot(v.own_t[...], one_hot(v.ids[0:1, cols], 0, ent)).astype(bf16)
-
-    def gather_tails(base, cols):
-        v.t[:, cols] = dot(v.par_t[...], one_hot(v.ids[2:3, cols], 0, ent)).astype(bf16)
+    def add_columns(which, places):
+        blocks, hots = [], []
+        for part, second, last in places:
+            blocks.append(v.table[part, which, second, last].reshape(COLUMN, width))
+            base = chunk_base(part, which, second) + last * COLUMN
+            hots.append(one_hot(v.ids[1:2, :], base, COLUMN))
+        v.w[...] += dot(jnp.concatenate(blocks, axis=0), jnp.concatenate(hots, axis=0), FIRST)
+
+    def add_early(which):
+        add_columns(
+            which,
+            [
+                (part, second, pos[LAST[part]])
+                for part in range(PARTS)
+                for second in range(FOUR)
+            ],
+        )
+
+    def others(step):
+        return [
+            (
+                part,
+                moved(pos, SECOND[part], -step)[SECOND[part]],
+                moved(pos, LAST[part], there)[LAST[part]],
+            )
+            for part in range(PARTS)
+            for there in range(1, FOUR)
+        ]
 
     def add(which, step):
-        @pl.loop(0, PARTS)
-        def _(part):
-            second = lax.rem(at_part(part, pos["y"], pos["x"]) - step + FOUR, FOUR)
-            block = v.table[part, which, second].reshape(CHUNK, width)
-            hot = one_hot(v.ids[1:2, :], chunk_base(part, which, second), CHUNK)
-            v.w[...] += dot(block, hot, FIRST)
-
+        add_columns(which, others(step))
+
+    early = []
+    for part in range(PARTS):
+        columns = v.table.at[part, core, :, pos[LAST[part]]]
+        early.append(put(columns, columns, sibling))
     across = []
 
     def cross(step):
-        chunks = []
         for part in range(PARTS):
             for copy in along_last[step][part]:
                 copy.wait_recv()
-            second = moved(pos, SECOND[part], -step)[SECOND[part]]
-            chunk = v.table.at[part, core, second]
-            chunks.append(put(chunk, chunk, sibling))
-        across.append(chunks)
+        columns = [v.table.at[part, core, second, last] for part, second, last in others(step)]
+        across.append([put(column, column, sibling) for column in columns])
 
     def add_across(step):
         for copy in across[step]:
             copy.wait_recv()
         add(1 - core, step)
 
-    tiles(gather_heads)
-    ones = jnp.ones((v.negs.shape[1], LANES), bf16)
-    for row in range(4):
-        v.count[row] = dot(one_hot(v.negs[row : row + 1, :], 0, ent), ones)
+    add_early(core)
     cross(0)
+    add(core, 0)
+    for copy in early:
+        copy.wait_recv()
     partner.turn("z_hi", "z_lo")
-    add(core, 0)
+    add_early(1 - core)
     cross(1)
+    add_across(0)
     mine = v.partner.at[x_low, core]
     mine[: rows // 2, :] = partner.take(0, "z_lo")
     mine[rows // 2 :, :] = partner.take(1, "z_lo")
     replicas = to_replicas(put, v.partner, pos, core)
-    add_across(0)
+    add(core, 1)
     cross(2)
-    add(core, 1)
     add_across(1)
+    add(core, 2)
     cross(3)
-    add(core, 2)
+    add_across(2)
+    add(core, 3)
+    add_across(3)
     for copy in replicas:
         copy.wait_recv()
     v.par_t[...] = v.partner[...].reshape(ent, width).astype(f32).T.astype(bf16)
     tiles(gather_tails)
-    add_across(2)
-    add(core, 3)
-    add_across(3)
 
     def edges(base, cols):
         slot = lax.broadcasted_iota(jnp.int32, (1, TILE), 1) + base
@@ -399,50 +431,51 @@
         rel_grad = jnp.concatenate(
             [qa * ha + qb * hb + pa * ta + pb * tb, qb * ha - qa * hb + pa * tb - pb * ta], axis=0
         )
-        v.rg[cols, :] = rel_grad.T.astype(bf16)
+        v.rg[:, cols] = rel_grad.astype(bf16)
         hot_h = one_hot(v.ids[0:1, cols], 0, ent)
         hot_t = one_hot(v.ids[2:3, cols], 0, ent)
-        v.head[...] += dot(head_w, probe_low, INNER) + dot(hot_h, head_grad.astype(bf16), INNER)
-        v.tail[...] += dot(tail_w, query_low, INNER) + dot(hot_t, tail_grad.astype(bf16), INNER)
+        v.head[...] += dot(
+            jnp.concatenate([probe_low, head_grad.astype(bf16)], axis=1),
+            jnp.concatenate([head_w, hot_h], axis=1),
+            INNER,
+        )
+        v.tail[...] += dot(
+            jnp.concatenate([query_low, tail_grad.astype(bf16)], axis=1),
+            jnp.concatenate([tail_w, hot_t], axis=1),
+            INNER,
+        )
 
     tiles(edges)
     shape = v.ent.shape[1:]
-    v.ent[0] = v.head[...].astype(bf16).reshape(shape)
-    v.ent[1] = v.tail[...].astype(bf16).reshape(shape)
+    v.ent[0] = v.head[...].T.astype(bf16).reshape(shape)
+    v.ent[1] = v.tail[...].T.astype(bf16).reshape(shape)
 
     ent_copy = put(v.ent.at[:, :, 1 - core], v.ent_core, sibling)
 
-    def chunk(part, which, step):
-        second = lax.rem(at_part(part, pos["y"], pos["x"]) + step, FOUR)
-        hot = one_hot(v.ids[1:2, :], chunk_base(part, which, second), CHUNK)
-        return dot(hot, v.rg[...])
+    def chunk(which, step, out, kind):
+        hots = []
+        for part in range(PARTS):
+            second = moved(pos, SECOND[part], step)[SECOND[part]]
+            hots.append(one_hot(v.ids[1:2, :], chunk_base(part, which, second), CHUNK))
+        summed = dot(v.rg[...], jnp.concatenate(hots, axis=0), INNER).astype(kind)
+        for column in range(PARTS * FOUR):
+            out[column] = summed[:, column * COLUMN : (column + 1) * COLUMN]
 
     def for_sibling(step):
-        @pl.loop(0, PARTS)
-        def _(part):
-            v.for_core[step, part] = chunk(part, 1 - core, step).astype(bf16)
-
+        chunk(1 - core, step, v.for_core.at[step], bf16)
         return put(v.for_core.at[step], v.from_core.at[step], sibling)
 
     def for_chips(step, core_copy):
-        @pl.loop(0, PARTS)
-        def _(part):
-            v.product[part] = chunk(part, core, step)
-
+        chunk(core, step, v.product, f32)
         core_copy.wait_recv()
-
-        @pl.loop(0, PARTS)
-        def _(part):
-            summed = v.product[part] + v.from_core[step, part].astype(f32)
-            v.total[step, part] = summed.astype(bf16).reshape(v.total.shape[2:])
-
+        v.total[step] = (v.product[...] + v.from_core[step].astype(f32)).astype(bf16)
         flying = []
         for part in range(PARTS):
             for there in range(1, FOUR):
                 target = moved(pos, LAST[part], there)
                 flying.append(
                     put(
-                        v.total.at[step, part, target[LAST[part]]],
+                        v.total.at[step, part * FOUR + target[LAST[part]]],
                         v.in_last.at[step, part, there - 1],
                         device(target, core),
                     )
@@ -450,7 +483,7 @@
         return flying
 
     def sum_last(step, part):
-        value = v.total[step, part, pos[LAST[part]]].astype(f32)
+        value = v.total[step, part * FOUR + pos[LAST[part]]].astype(f32)
         for there in range(FOUR - 1):
             value += v.in_last[step, part, there].astype(f32)
         return value
@@ -477,24 +510,23 @@
     side_copy = put(v.ent_half.at[:, 1 - x_low], v.ent_side, device(beside(pos), core))
     flying_1 = for_chips(1, core_copy)
     core_copy = for_sibling(2)
+    flying_2 = for_chips(2, core_copy)
     side_copy.wait_recv()
     piece = (v.ent_half[1, x_low].astype(f32) + v.ent_side[1].astype(f32)).astype(bf16)
     partner.send(0, "z_hi", piece[: rows // 2])
     partner.send(1, "z_hi", piece[rows // 2 :])
-    flying_2 = for_chips(2, core_copy)
+    core_copy = for_sibling(3)
     seconds = to_second(1, flying_1)
-    core_copy = for_sibling(3)
+    flying_3 = for_chips(3, core_copy)
+    core_copy = for_sibling(0)
+    seconds += to_second(2, flying_2)
+    flying_0 = for_chips(0, core_copy)
     partner.turn("z_hi", "z_lo")
-    flying_3 = for_chips(3, core_copy)
-    seconds += to_second(2, flying_2)
-    partner.turn("z_lo", "y")
-    core_copy = for_sibling(0)
-    flying_0 = for_chips(0, core_copy)
-    partner.turn("y", "x")
     seconds += to_second(3, flying_3)
     for copy in flying_0:
         copy.wait_recv()
     own = [sum_last(0, part) for part in range(PARTS)]
+    partner.turn("z_lo", "y")
     for copy in seconds:
         copy.wait_recv()
     last_z = []
@@ -502,7 +534,7 @@
         value = own[part]
         for step in range(FOUR - 1):
             value += v.in_second[step, part].astype(f32)
-        v.three[part] = value.astype(bf16)
+        v.three[part] = value.T.astype(bf16).reshape(v.three.shape[1:])
         for step in range(1, NZ):
             target = moved(pos, "z", step)
             last_z.append(
@@ -512,6 +544,7 @@
                     device(target, core),
                 )
             )
+    partner.turn("y", "x")
     mine = ent_sum_ref.at[x_low, core]
     held = v.ent_half[0, x_low].astype(f32) + v.ent_side[0].astype(f32)
     for side in range(2):

time: 123 us -> 116 us (0.943)
  Pallas kernels: 114 us -> 107 us
    pallas_call x1, Pallas kernels: 114 us -> 107 us  [whole_round(): pl.pallas_call(functools.partial(round_kernel, scratch, block_rows, sampl...]
where the time goes in v3:
time: 116 us; the launch traced here: 115 us
  Pallas kernels  107 us (92%)
  other arithmetic  5.59 us (5%)
  between operations  1.35 us (1%)
  local copies, waits for them, and re-layouts  1.24 us (1%)
    pallas_call x1, Pallas kernels, whole_round(): pl.pallas_call(functools.partial(round_kernel, scratch, block_rows, sampl...  107 us

profile of v3, /device:TPU:1, one launch (start us, length us, event | category | flops | bytes accessed | tf_op | source)
XLA Modules:
  0.0 115.5 jit_solution(14020070500738545734)
XLA Ops:
  0.6 0.0 copy-start.4
  0.6 0.0 copy-start.3
  0.7 0.8 fusion.8
  1.4 0.0 copy-done.4
  1.4 0.0 copy-done.3
  1.4 0.6 pad_add_fusion.refs_2_
  2.7 107.3 %shard_map.138 = (f32[2,16,384]{2,1,0:T(8,128)}, bf16[2,2,128,384]{3,2,1,0:T(8,128)(2,1)}) custom-call(s32[64]{0:T(128)} %refs_0_.1, s32[1]{0:T(128)S(6)} %min.3.refs_1_, s32[3,2000]{1,0:T(4,128)} %pad_add_fusion.refs_2_, s32[2,1000]{1,0:T(2,128)} %refs_3_.1, s32[2,1000]{1,0:T(2,128)} %refs_4_.1, f32[29,384]{1,0:T(8,128)} %refs_5_.1, f32[512,384]{1,0:T(8,128)} %refs_6_.1), custom_call_target="tpu_custom_call" | custom-call | tf_op jit(solution)/shard_map/pallas_call | solution.py:573
  110.0 0.0 copy-start
  110.0 1.2 %fusion = (f32[2,2,128]{2,1,0:T(2,128)S(1)}, f32[2,2,128,384]{3,2,1,0:T(8,128)S(1)}) fusion(bf16[2,2,128,384]{3,2,1,0:T(8,128)(2,1)} %get-tuple-element.6), kind=kLoop, calls=%fused_computation.2 | loop fusion | flops 785920 | bytes 1181696 | tf_op jit(solution)/shard_map/reduce_sum | solution.py:589
  111.3 0.0 copy-start.5
  111.3 0.7 copy-done.5
  112.0 0.6 fusion.29
  112.5 0.0 copy-done
  112.5 0.0 copy-start.1
  112.5 1.0 fusion.1
  113.6 0.0 copy-start.2
  113.6 0.0 copy-done.1
  113.6 0.0 copy-start.6
  113.6 0.1 multiply_reduce_fusion
  113.7 0.6 copy-done.6
  114.2 0.5 fusion.28
  114.8 0.0 copy-done.2
  114.8 0.7 divide_subtract_fusion
  (1 shorter events, 0.0 us)
Async XLA Ops:
  0.6 0.8 copy-start.4
  0.6 0.8 copy-start.3
  110.0 2.5 %copy-start = (f32[512,384]{1,0:T(8,128)S(1)}, f32[512,384]{1,0:T(8,128)}, u32[]{:S(2)}) copy-start(f32[512,384]{1,0:T(8,128)} %refs_6_.1) | copy-start | bytes 2359300
  111.3 0.7 copy-start.5
  112.5 1.0 copy-start.1
  113.6 1.2 %copy-start.2 = (f32[29,384]{1,0:T(8,128)S(1)}, f32[29,384]{1,0:T(8,128)}, u32[]{:S(2)}) copy-start(f32[29,384]{1,0:T(8,128)} %refs_5_.1) | copy-start | bytes 133636
  113.6 0.7 copy-start.6

commit v4 on v3

--- a/solution.py
+++ b/solution.py
@@ -17,7 +17,7 @@
 VMEM_LIMIT = 56 * 1024 * 1024
 COLUMN = NZ * HALF
 CHUNK = FOUR * COLUMN
-TILE = 512
+TILE = 1024
 LANES = 128
 INNER = (((1,), (1,)), ((), ()))
 FIRST = (((0,), (0,)), ((), ()))
@@ -152,8 +152,8 @@
         ]
 
 
-def to_replicas(put, whole, pos, core):
-    mine = whole.at[lax.rem(pos["x"], 2), core]
+def to_replicas(put, whole, pos, core, some):
+    mine = whole.at[lax.rem(pos["x"], 2), core, some]
     others = [device(beside(pos), core), device(beside(pos), 1 - core), device(pos, 1 - core)]
     return [put(mine, mine, target) for target in others]
 
@@ -378,10 +378,11 @@
     add_early(1 - core)
     cross(1)
     add_across(0)
-    mine = v.partner.at[x_low, core]
-    mine[: rows // 2, :] = partner.take(0, "z_lo")
-    mine[rows // 2 :, :] = partner.take(1, "z_lo")
-    replicas = to_replicas(put, v.partner, pos, core)
+    replicas = []
+    for side in range(2):
+        some = pl.ds(side * (rows // 2), rows // 2)
+        v.partner[x_low, core, some, :] = partner.take(side, "z_lo")
+        replicas += to_replicas(put, v.partner, pos, core, some)
     add(core, 1)
     cross(2)
     add_across(1)
@@ -450,7 +451,9 @@
     v.ent[0] = v.head[...].T.astype(bf16).reshape(shape)
     v.ent[1] = v.tail[...].T.astype(bf16).reshape(shape)
 
-    ent_copy = put(v.ent.at[:, :, 1 - core], v.ent_core, sibling)
+    ent_copies = {
+        side: put(v.ent.at[side, :, 1 - core], v.ent_core.at[side], sibling) for side in (1, 0)
+    }
 
     def chunk(which, step, out, kind):
         hots = []
@@ -505,16 +508,22 @@
 
     partner = Partner(copies, pos, core, plan_ref[0], v.back)
     core_copy = for_sibling(1)
-    ent_copy.wait_recv()
-    v.ent_half[...] = (v.ent[:, :, core].astype(f32) + v.ent_core[...].astype(f32)).astype(bf16)
-    side_copy = put(v.ent_half.at[:, 1 - x_low], v.ent_side, device(beside(pos), core))
+    side_copies = {}
+    for side in (1, 0):
+        ent_copies[side].wait_recv()
+        v.ent_half[side] = (
+            v.ent[side, :, core].astype(f32) + v.ent_core[side].astype(f32)
+        ).astype(bf16)
+        side_copies[side] = put(
+            v.ent_half.at[side, 1 - x_low], v.ent_side.at[side], device(beside(pos), core)
+        )
     flying_1 = for_chips(1, core_copy)
     core_copy = for_sibling(2)
-    flying_2 = for_chips(2, core_copy)
-    side_copy.wait_recv()
+    side_copies[1].wait_recv()
     piece = (v.ent_half[1, x_low].astype(f32) + v.ent_side[1].astype(f32)).astype(bf16)
     partner.send(0, "z_hi", piece[: rows // 2])
     partner.send(1, "z_hi", piece[rows // 2 :])
+    flying_2 = for_chips(2, core_copy)
     core_copy = for_sibling(3)
     seconds = to_second(1, flying_1)
     flying_3 = for_chips(3, core_copy)
@@ -545,12 +554,16 @@
                 )
             )
     partner.turn("y", "x")
-    mine = ent_sum_ref.at[x_low, core]
+    side_copies[0].wait_recv()
     held = v.ent_half[0, x_low].astype(f32) + v.ent_side[0].astype(f32)
+    replicas = []
     for side in range(2):
-        some = slice(side * (rows // 2), (side + 1) * (rows // 2))
-        mine[some, :] = (held[some] + partner.take(side, "x").astype(f32)).astype(bf16)
-    replicas = to_replicas(put, ent_sum_ref, pos, core)
+        some = pl.ds(side * (rows // 2), rows // 2)
+        ours = held[side * (rows // 2) : (side + 1) * (rows // 2)]
+        ent_sum_ref[x_low, core, some, :] = (
+            ours + partner.take(side, "x").astype(f32)
+        ).astype(bf16)
+        replicas += to_replicas(put, ent_sum_ref, pos, core, some)
     for copy in last_z:
         copy.wait_recv()
     for part in range(PARTS):

time: 116 us -> 114 us (0.983)
  Pallas kernels: 107 us -> 105 us
    pallas_call x1, Pallas kernels: 107 us -> 105 us  [whole_round(): pl.pallas_call(functools.partial(round_kernel, scratch, block_rows, sampl...]
where the time goes in v4:
time: 114 us
  Pallas kernels  105 us (92%)
  other arithmetic  5.59 us (5%)
  between operations  1.35 us (1%)
  local copies, waits for them, and re-layouts  1.24 us (1%)
    pallas_call x1, Pallas kernels, whole_round(): pl.pallas_call(functools.partial(round_kernel, scratch, block_rows, sampl...  105 us

profile of v4, /device:TPU:1, one launch (start us, length us, event | category | flops | bytes accessed | tf_op | source)
XLA Modules:
  0.0 113.5 jit_solution(10940458871486043530)
XLA Ops:
  0.6 0.0 copy-start.4
  0.6 0.0 copy-start.3
  0.7 0.8 fusion.8
  1.4 0.0 copy-done.4
  1.4 0.0 copy-done.3
  1.4 0.6 pad_add_fusion.refs_2_
  2.7 105.4 %shard_map.138 = (f32[2,16,384]{2,1,0:T(8,128)}, bf16[2,2,128,384]{3,2,1,0:T(8,128)(2,1)}) custom-call(s32[64]{0:T(128)} %refs_0_.1, s32[1]{0:T(128)S(6)} %min.3.refs_1_, s32[3,2000]{1,0:T(4,128)} %pad_add_fusion.refs_2_, s32[2,1000]{1,0:T(2,128)} %refs_3_.1, s32[2,1000]{1,0:T(2,128)} %refs_4_.1, f32[29,384]{1,0:T(8,128)} %refs_5_.1, f32[512,384]{1,0:T(8,128)} %refs_6_.1), custom_call_target="tpu_custom_call" | custom-call | tf_op jit(solution)/shard_map/pallas_call | solution.py:586
  108.1 0.0 copy-start
  108.1 1.2 %fusion = (f32[2,2,128]{2,1,0:T(2,128)S(1)}, f32[2,2,128,384]{3,2,1,0:T(8,128)S(1)}) fusion(bf16[2,2,128,384]{3,2,1,0:T(8,128)(2,1)} %get-tuple-element.6), kind=kLoop, calls=%fused_computation.2 | loop fusion | flops 785920 | bytes 1181696 | tf_op jit(solution)/shard_map/reduce_sum | solution.py:602
  109.4 0.0 copy-start.5
  109.4 0.7 copy-done.5
  110.0 0.6 fusion.29
  110.6 0.0 copy-done
  110.6 0.0 copy-start.1
  110.6 1.0 fusion.1
  111.7 0.0 copy-start.2
  111.7 0.0 copy-done.1
  111.7 0.0 copy-start.6
  111.7 0.1 multiply_reduce_fusion
  111.8 0.6 copy-done.6
  112.3 0.5 fusion.28
  112.8 0.0 copy-done.2
  112.8 0.7 divide_subtract_fusion
  (1 shorter events, 0.0 us)
Async XLA Ops:
  0.6 0.8 copy-start.4
  0.6 0.8 copy-start.3
  108.1 2.5 %copy-start = (f32[512,384]{1,0:T(8,128)S(1)}, f32[512,384]{1,0:T(8,128)}, u32[]{:S(2)}) copy-start(f32[512,384]{1,0:T(8,128)} %refs_6_.1) | copy-start | bytes 2359300
  109.4 0.7 copy-start.5
  110.6 1.0 copy-start.1
  111.7 1.2 %copy-start.2 = (f32[29,384]{1,0:T(8,128)S(1)}, f32[29,384]{1,0:T(8,128)}, u32[]{:S(2)}) copy-start(f32[29,384]{1,0:T(8,128)} %refs_5_.1) | copy-start | bytes 133636
  111.7 0.7 copy-start.6
